TPU v7x, 32 devices: a whole 2x2x4 slice. The times are simulated.
32 devices in a mesh: kv: 4 (over y, x), blk: 8 (over z, core).
Axes of the slice: x: 2, y: 2, z: 4, core: 2. Of those that a mesh axis runs over, the one named last changes fastest.
Arguments:
- embeds: bfloat16 [3, 64, 4096], P(None, None, 'blk'), may hold values from -6 to 6
- attn_gain: float32 [4096], P('blk'), may hold values from 0.25 to 1.75
- w_query: bfloat16 [4096, 4096], P('blk', 'kv'), may hold values from -0.1875 to 0.1875
- w_key: bfloat16 [4096, 512], P('blk', 'kv'), may hold values from -0.09375 to 0.09375
- w_value: bfloat16 [4096, 512], P('blk', 'kv'), may hold values from -0.09375 to 0.09375
- w_out: bfloat16 [4096, 4096], P('kv', 'blk'), may hold values from -0.375 to 0.375
- cache_kv: bfloat16 [256, 4, 2, 128, 128], P('blk', 'kv'), may hold values from -102 to 102, as said below
- lengths: int32 [64], replicated, may hold values from 1 to 8192, as said below
- block_table: int32 [64, 64], replicated, may hold values from 0 to 256, as said below
- parents: int32 [3, 64], replicated, may hold values from 0 to 63, as said below
Outputs:
- out_rows: bfloat16 [3, 64, 4096], P(None, None, 'blk')
- appended: bfloat16 [3, 64, 4, 2, 128], P(None, 'blk', 'kv')
Inputs may be any that keep to these rules, and one draw needn't show every extreme that they name: `lengths`: one beam holds exactly 8192 tokens. `block_table`: row b names the slots of beam b's blocks of 128 tokens in order; entries at and past ceil(lengths[b] / 128) equal 256; no slot is named twice. parents[s, b] lies in the aligned group of 8 beams that holds b. `cache_kv`: slots that no row of block_table names are never read.
All inputs are finite; a program needn't handle non-finite values.
Results may differ from a plain program's by a relative error of at most 0.0044.
The roundings to bfloat16 on the way count: a program that leaves them out, or rounds other values in their place, can miss the bound.
Values may be sent and summed in bfloat16 or wider, within the bound.
A program may use at most 64 MiB of HBM per device.

v0:
```python
import math

import jax
import jax.numpy as jnp
from jax import lax
from jax.sharding import PartitionSpec as P

GROUP = 8


NEGATIVE = -1e30
EPSILON = 1e-05
ROPE_BASE = 5000000.0


def rotate(vector, position):
    half_dim = vector.shape[-1] // 2
    exponent = jnp.arange(half_dim, dtype=jnp.float32) * (2.0 / vector.shape[-1])
    frequency = ROPE_BASE ** (-exponent)
    angles = position.astype(jnp.float32)[:, None] * frequency[None, :]
    target_shape = (position.shape[0],) + (1,) * (vector.ndim - 2) + (half_dim,)
    cosines = jnp.cos(angles).reshape(target_shape)
    sine_part = jnp.sin(angles).reshape(target_shape)
    first_half = vector[..., :half_dim]
    second_half = vector[..., half_dim:]
    return jnp.concatenate(
        [
            first_half * cosines - second_half * sine_part,
            second_half * cosines + first_half * sine_part,
        ],
        axis=-1,
    )


def body(
    embeds, attn_gain, w_query, w_key, w_value, w_out, cache_kv, lengths, block_table, parents
):
    axis_count = lax.axis_size("blk")
    shard_index = lax.axis_index("blk")
    step_total, beam_count, width_part = embeds.shape
    beams_here = beam_count // axis_count
    slot_count = cache_kv.shape[0]
    total_slots = slot_count * axis_count
    block_len = cache_kv.shape[3]
    head_dim = cache_kv.shape[4]
    heads_per_group = w_query.shape[1] // head_dim
    group_count = beam_count // GROUP
    model_width = width_part * axis_count
    scaling = 1.0 / math.sqrt(head_dim)
    row_offset = shard_index * beams_here
    joined_weights = jnp.concatenate([w_query, w_key, w_value], axis=1)
    cached_keys = cache_kv[:, 0, 0]
    cached_values = cache_kv[:, 0, 1]
    max_blocks = block_table.shape[1]
    beam_ids = jnp.broadcast_to(jnp.arange(beam_count, dtype=jnp.int32)[:, None], block_table.shape)
    block_ids = jnp.broadcast_to(
        jnp.arange(max_blocks, dtype=jnp.int32)[None, :], block_table.shape
    )
    flat_table = block_table.reshape(-1)
    owner_all = jnp.full((total_slots + 1,), -1, jnp.int32).at[flat_table].set(beam_ids.reshape(-1))
    logical_all = jnp.zeros((total_slots + 1,), jnp.int32).at[flat_table].set(block_ids.reshape(-1))
    owner_beam = lax.dynamic_slice_in_dim(owner_all, shard_index * slot_count, slot_count)
    logical_block = lax.dynamic_slice_in_dim(logical_all, shard_index * slot_count, slot_count)
    filled = owner_beam >= 0
    safe_owner = jnp.maximum(owner_beam, 0)
    group_of = safe_owner // GROUP
    group_onehot = (
        (group_of[:, None] == jnp.arange(group_count, dtype=jnp.int32)[None, :]) & filled[:, None]
    ).astype(jnp.float32)
    token_index = jnp.arange(block_len, dtype=jnp.int32)
    in_length = (
        logical_block[:, None] * block_len + token_index[None, :] < lengths[safe_owner][:, None]
    )
    members = group_of[:, None] * GROUP + jnp.arange(GROUP, dtype=jnp.int32)[None, :]
    root_beams = jnp.arange(beam_count, dtype=jnp.int32)
    new_keys = jnp.zeros((step_total, beams_here, head_dim), jnp.bfloat16)
    new_values = jnp.zeros((step_total, beams_here, head_dim), jnp.bfloat16)
    outputs = []
    for step_index in range(step_total):
        root_beams = root_beams[parents[step_index]]
        local_parent = (
            lax.dynamic_slice_in_dim(parents[step_index], row_offset, beams_here) - row_offset
        )
        new_keys = new_keys[:, local_parent]
        new_values = new_values[:, local_parent]
        stream = embeds[step_index].astype(jnp.float32)
        squares = lax.psum(jnp.sum(stream * stream, axis=1), "blk")
        inverse_rms = lax.rsqrt(squares / model_width + EPSILON)
        normed = (stream * inverse_rms[:, None] * attn_gain[None, :]).astype(jnp.bfloat16)
        projected = lax.psum_scatter(
            jnp.dot(normed, joined_weights, preferred_element_type=jnp.float32),
            "blk",
            scatter_dimension=0,
            tiled=True,
        )
        position = (
            lax.dynamic_slice_in_dim(lengths[root_beams], row_offset, beams_here) + step_index
        )
        rotated_query = rotate(
            projected[:, : heads_per_group * head_dim].reshape(
                beams_here, heads_per_group, head_dim
            ),
            position,
        ).astype(jnp.bfloat16)
        key_new = rotate(
            projected[:, heads_per_group * head_dim : (heads_per_group + 1) * head_dim], position
        ).astype(jnp.bfloat16)
        value_new = projected[:, (heads_per_group + 1) * head_dim :].astype(jnp.bfloat16)
        new_keys = new_keys.at[step_index].set(key_new)
        new_values = new_values.at[step_index].set(value_new)
        queries = lax.all_gather(
            rotated_query.reshape(beams_here, heads_per_group * head_dim), "blk", axis=0, tiled=True
        )
        slot_query = queries.reshape(group_count, GROUP * heads_per_group, head_dim)[group_of]
        scores = (
            jnp.einsum("sqd,skd->sqk", slot_query, cached_keys, preferred_element_type=jnp.float32)
            * scaling
        )
        scores = scores.reshape(slot_count, GROUP, heads_per_group, block_len)
        active = ((root_beams[members] == owner_beam[:, None])[:, :, None] & in_length[:, None, :])[
            :, :, None, :
        ]
        slot_top = jnp.max(jnp.where(active, scores, NEGATIVE), axis=-1)
        group_top = jnp.max(
            jnp.where(group_onehot[:, :, None, None] > 0, slot_top[:, None], NEGATIVE), axis=0
        ).reshape(beam_count, heads_per_group)
        latest_key_rows = new_keys[: step_index + 1]
        new_scores = (
            jnp.einsum(
                "pam,fpm->paf", rotated_query, latest_key_rows, preferred_element_type=jnp.float32
            )
            * scaling
        )
        own_top = jnp.maximum(
            lax.dynamic_slice_in_dim(group_top, row_offset, beams_here),
            jnp.max(new_scores, axis=-1),
        )
        local_top = lax.dynamic_update_slice_in_dim(group_top, own_top, row_offset, 0)
        ceiling = lax.pmax(local_top, "blk")
        slot_ceiling = ceiling.reshape(group_count, GROUP, heads_per_group)[group_of]
        prob_weights = jnp.exp(jnp.where(active, scores - slot_ceiling[..., None], NEGATIVE))
        slot_denominator = jnp.sum(prob_weights, axis=-1)
        slot_numer = jnp.einsum(
            "sgqk,skd->sgqd",
            prob_weights.astype(jnp.bfloat16),
            cached_values,
            preferred_element_type=jnp.float32,
        )
        numerator = jnp.einsum(
            "sg,sx->gx",
            group_onehot,
            slot_numer.reshape(slot_count, -1),
            precision=lax.Precision.HIGHEST,
        ).reshape(beam_count, heads_per_group, head_dim)
        denominator = jnp.einsum(
            "sg,sx->gx",
            group_onehot,
            slot_denominator.reshape(slot_count, -1),
            precision=lax.Precision.HIGHEST,
        ).reshape(beam_count, heads_per_group)
        own_ceiling = lax.dynamic_slice_in_dim(ceiling, row_offset, beams_here)
        new_weights = jnp.exp(new_scores - own_ceiling[..., None])
        updated_denominator = jnp.sum(new_weights, axis=-1)
        new_numer = jnp.einsum(
            "pjz,zpc->pjc",
            new_weights.astype(jnp.bfloat16),
            new_values[: step_index + 1],
            preferred_element_type=jnp.float32,
        )
        numerator, denominator = (
            lax.psum_scatter(numerator, "blk", scatter_dimension=0, tiled=True),
            lax.psum_scatter(denominator, "blk", scatter_dimension=0, tiled=True),
        )
        own_rows = (
            ((numerator + new_numer) / (denominator + updated_denominator)[..., None])
            .astype(jnp.bfloat16)
            .reshape(beams_here, heads_per_group * head_dim)
        )
        attended = lax.all_gather(own_rows, "blk", axis=0, tiled=True)
        partial_value = jnp.dot(attended, w_out, preferred_element_type=jnp.float32)
        head_total = lax.psum(partial_value, "kv")
        outputs.append((stream + head_total).astype(jnp.bfloat16))
    appended = jnp.stack([new_keys, new_values], axis=2)[:, :, None]
    return (jnp.stack(outputs), appended)


def solution(mesh):
    return jax.shard_map(
        body,
        mesh=mesh,
        in_specs=(
            P(None, None, "blk"),
            P("blk"),
            P("blk", "kv"),
            P("blk", "kv"),
            P("blk", "kv"),
            P("kv", "blk"),
            P("blk", "kv", None, None, None),
            P(),
            P(),
            P(),
        ),
        out_specs=(P(None, None, "blk"), P(None, "blk", "kv", None, None)),
        check_vma=False,
    )
```

profile of v0, /device:TPU:0, one launch (start us, length us, event | category | flops | bytes accessed | tf_op | source)
XLA Modules:
  0.0 408.7 jit_solution(14329089226652416182)
XLA Ops:
  8.4 18.1 %all-reduce.4 = (f32[64]{0:T(128)S(1)}, f32[64]{0:T(128)S(1)}, f32[64]{0:T(128)S(1)}) all-reduce(f32[64]{0:T(128)S(1)} %get-tuple-element.86, f32[64]{0:T(128)S(1)} %get-tuple-element.85, f32[64]{0:T(128)S(1)} %get-tuple-element.84), channel_id=1, replica_groups=mesh['kv'=4,'blk'=8] {'blk'}, use_global_device_ids=true, to_apply=%region_25.26 | all-reduce | flops 192 | bytes 1536 | tf_op jit(solution)/shard_map/psum | solution.py:87
  26.5 1.3 constant_dynamic-update-slice_fusion.2
  34.3 15.5 %scatter_custom_fusion = s32[257]{0:T(512)S(1)} fusion(s32[4096]{0:T(1024)S(1)} %bitcast.297, s32[4096]{0:T(1024)S(1)} %reshape.1134, s32[]{:T(128)} %constant.196.clone.1), kind=kCustom, calls=%fused_computation.267 | custom fusion | bytes 1032 | tf_op jit(solution)/shard_map/scatter | solution.py:60
  50.0 1.9 gather_fusion.15
  51.9 1.9 gather_fusion.7
  53.8 1.9 gather_fusion.1
  59.2 15.5 %scatter_custom_fusion.1 = s32[257]{0:T(512)S(1)} fusion(s32[4096]{0:T(1024)S(1)} %bitcast.298, s32[4096]{0:T(1024)S(1)} %reshape.1142, s32[]{:T(128)} %constant.197.clone.1), kind=kCustom, calls=%fused_computation.265 | custom fusion | bytes 1032 | tf_op jit(solution)/shard_map/scatter | solution.py:61
  78.7 10.3 %reduce-scatter.15.cloned.1.call-done = f32[8,1280]{1,0:T(8,128)} async-done(((f32[64,1280]{1,0:T(8,128)}), f32[8,1280]{1,0:T(8,128)}) %reduce-scatter.15.cloned.1.call-update) | async-done | bytes 40976 | tf_op jit(solution)/shard_map/reduce_scatter | solution.py:90
  89.0 30.9 %reduce-scatter.11.cloned.1.call-done = f32[8,1280]{1,0:T(8,128)} async-done(((f32[64,1280]{1,0:T(8,128)}), f32[8,1280]{1,0:T(8,128)}) %reduce-scatter.11.cloned.1.call-update) | async-done | bytes 40976 | tf_op jit(solution)/shard_map/reduce_scatter | solution.py:90
  124.1 1.3 fusion.139
  127.6 1.4 fusion.163
  131.8 14.0 %all_gather.20 = bf16[64,1024]{1,0:T(8,128)(2,1)S(1)} all-gather(bf16[8,1024]{1,0:T(8,128)(2,1)S(1)} %bitcast.285), channel_id=1, replica_groups=mesh['kv'=4,'blk'=8] {'blk'}, dimensions={0}, use_global_device_ids=true | all-gather | bytes 147456 | tf_op jit(solution)/shard_map/all_gather | solution.py:111
  145.8 14.0 %all_gather.22 = bf16[64,1024]{1,0:T(8,128)(2,1)S(1)} all-gather(bf16[8,1024]{1,0:T(8,128)(2,1)S(1)} %bitcast.284), channel_id=1, replica_groups=mesh['kv'=4,'blk'=8] {'blk'}, dimensions={0}, use_global_device_ids=true | all-gather | bytes 147456 | tf_op jit(solution)/shard_map/all_gather | solution.py:111
  159.8 14.0 %all_gather.18 = bf16[64,1024]{1,0:T(8,128)(2,1)S(1)} all-gather(bf16[8,1024]{1,0:T(8,128)(2,1)S(1)} %fusion.187), channel_id=1, replica_groups=mesh['kv'=4,'blk'=8] {'blk'}, dimensions={0}, use_global_device_ids=true | all-gather | bytes 147456 | tf_op jit(solution)/shard_map/all_gather | solution.py:111
  173.9 1.4 gather_fusion.4
  175.3 1.7 gather_fusion.17
  177.0 1.5 gather_fusion.9
  178.5 2.8 fusion.9
  181.5 2.9 fusion.12
  184.5 2.8 fusion.6
  187.9 27.1 %all-reduce.5 = (f32[64,8]{1,0:T(8,128)S(1)}, f32[64,8]{1,0:T(8,128)S(1)}, f32[64,8]{1,0:T(8,128)S(1)}) all-reduce(f32[64,8]{1,0:T(8,128)S(1)} %maximum_dynamic-update-slice_fusion, f32[64,8]{1,0:T(8,128)S(1)} %maximum_dynamic-update-slice_fusion.1, ...), channel_id=1, replica_groups=mesh['kv'=4,'blk'=8] {'blk'}, use_global_device_ids=true, to_apply=%region_30.31 | all-reduce | flops 1536 | bytes 12288 | tf_op jit(solution)/shard_map/pmax | solution.py:139
  215.9 1.8 fusion.28
  221.0 1.3 reshape.937
  223.2 1.8 fusion.24
  229.9 1.8 fusion.26
  235.4 27.0 %all-reduce.3 = (f32[64,8]{1,0:T(8,128)S(1)}, f32[64,8]{1,0:T(8,128)S(1)}, f32[64,8]{1,0:T(8,128)S(1)}) all-reduce(f32[64,8]{1,0:T(8,128)S(1)} %reshape.957, f32[64,8]{1,0:T(8,128)S(1)} %reshape.947, f32[64,8]{1,0:T(8,128)S(1)} %copy-done.12), channel_id=10, replica_groups=mesh['kv'=4,'blk'=8] {'blk'}, use_global_device_ids=true, to_apply=%region_33.34.clone | all-reduce | flops 1536 | bytes 12288
  263.4 17.1 %reduce-scatter.13.cloned.1.call-done = f32[8,8,128]{2,1,0:T(8,128)} async-done(((f32[64,8,128]{2,1,0:T(8,128)}), f32[8,8,128]{2,1,0:T(8,128)}) %reduce-scatter.13.cloned.1.call-update) | async-done | bytes 32784 | tf_op jit(solution)/shard_map/reduce_scatter | solution.py:171
  281.5 29.8 %reduce-scatter.17.cloned.1.call-done = f32[8,8,128]{2,1,0:T(8,128)} async-done(((f32[64,8,128]{2,1,0:T(8,128)}), f32[8,8,128]{2,1,0:T(8,128)}) %reduce-scatter.17.cloned.1.call-update) | async-done | bytes 32784 | tf_op jit(solution)/shard_map/reduce_scatter | solution.py:171
  312.3 14.0 %all_gather.23 = bf16[64,1024]{1,0:T(8,128)(2,1)S(1)} all-gather(bf16[8,1024]{1,0:T(8,128)(2,1)S(1)} %bitcast.286), channel_id=1, replica_groups=mesh['kv'=4,'blk'=8] {'blk'}, dimensions={0}, use_global_device_ids=true | all-gather | bytes 147456 | tf_op jit(solution)/shard_map/all_gather | solution.py:179
  326.2 14.0 %all_gather.21 = bf16[64,1024]{1,0:T(8,128)(2,1)S(1)} all-gather(bf16[8,1024]{1,0:T(8,128)(2,1)S(1)} %bitcast.283), channel_id=1, replica_groups=mesh['kv'=4,'blk'=8] {'blk'}, dimensions={0}, use_global_device_ids=true | all-gather | bytes 147456 | tf_op jit(solution)/shard_map/all_gather | solution.py:179
  342.1 14.0 %all_gather.19 = bf16[64,1024]{1,0:T(8,128)(2,1)S(1)} all-gather(bf16[8,1024]{1,0:T(8,128)(2,1)S(1)} %bitcast.282), channel_id=1, replica_groups=mesh['kv'=4,'blk'=8] {'blk'}, dimensions={0}, use_global_device_ids=true | all-gather | bytes 147456 | tf_op jit(solution)/shard_map/all_gather | solution.py:179
  357.7 42.3 %all-reduce.9.cloned.1.call-done = (f32[64,512]{1,0:T(8,128)}, f32[64,512]{1,0:T(8,128)}, f32[64,512]{1,0:T(8,128)}) async-done(((f32[64,512]{1,0:T(8,128)}, f32[64,512]{1,0:T(8,128)}, f32[64,512]{1,0:T(8,128)}), (f32[64,512]{1,0:T(8,128)}, f32[64,512]{1,0:T(8,128)}, f32[64,512]{1,0:T(8,128)})) %all-reduce.9.cloned.1.call-update) | async-done | bytes 393232 | tf_op jit(solution)/shard_map/psum | solution.py:181
  (250 shorter events, 45.9 us)
Async XLA Ops:
  7.2 333.0 %copy-start = (bf16[1024,512]{1,0:T(8,128)(2,1)S(1)}, bf16[1024,512]{1,0:T(8,128)(2,1)}, u32[]{:S(2)}) copy-start(bf16[1024,512]{1,0:T(8,128)(2,1)} %param.27) | copy-start | bytes 3145732
  7.2 20.7 %copy-start.13 = (bf16[512,128]{1,0:T(8,128)(2,1)S(1)}, bf16[512,128]{1,0:T(8,128)(2,1)}, u32[]{:S(2)}) copy-start(bf16[512,128]{1,0:T(8,128)(2,1)} %param.25) | copy-start | bytes 393220
  7.2 20.7 %copy-start.14 = (bf16[512,128]{1,0:T(8,128)(2,1)S(1)}, bf16[512,128]{1,0:T(8,128)(2,1)}, u32[]{:S(2)}) copy-start(bf16[512,128]{1,0:T(8,128)(2,1)} %param.26) | copy-start | bytes 393220
  7.2 70.8 %reduce-scatter.7.cloned.1.call-start = ((), (), s32[]{:S(2)}) async-start(), calls=%async_computation.6 | async-start | bytes 368640 | tf_op jit(solution)/shard_map/reduce_scatter | solution.py:90
  29.1 59.9 %reduce-scatter.15.cloned.1.call-start = ((), (), s32[]{:S(2)}) async-start(), calls=%async_computation.10 | async-start | bytes 368640 | tf_op jit(solution)/shard_map/reduce_scatter | solution.py:90
  30.3 89.6 %reduce-scatter.11.cloned.1.call-start = ((), (), s32[]{:S(2)}) async-start(), calls=%async_computation.8 | async-start | bytes 368640 | tf_op jit(solution)/shard_map/reduce_scatter | solution.py:90
  31.5 231.0 %reduce-scatter.9.cloned.1.call-start = ((), (), s32[]{:S(2)}) async-start(), calls=%async_computation.7 | async-start | bytes 294912 | tf_op jit(solution)/shard_map/reduce_scatter | solution.py:171
  49.8 27.3 %copy-start.17 = (pred[32]{0:T(512)(128)(4,1)}, pred[32]{0:T(512)(128)(4,1)S(1)}, u32[]{:S(2)}) copy-start(pred[32]{0:T(512)(128)(4,1)S(1)} %get-tuple-element.102) | copy-start | bytes 100
  49.9 27.3 %copy-start.21 = (s32[32]{0:T(128)}, s32[32]{0:T(128)S(1)}, u32[]{:S(2)}) copy-start(s32[32]{0:T(128)S(1)} %get-tuple-element.105) | copy-start | bytes 388
  55.7 20.1 %copy-start.41 = (u32[32]{0:T(128)S(1)}, u32[32]{0:T(128)}, u32[]{:S(2)}) copy-start(u32[32]{0:T(128)} %constant.220) | copy-start | bytes 388
  74.8 99.1 %copy-start.35 = (s32[1024]{0:T(1024)}, s32[1024]{0:T(1024)S(1)}, u32[]{:S(2)}) copy-start(s32[1024]{0:T(1024)S(1)} %pad_clamp_fusion.7) | copy-start | bytes 12292
  77.9 103.5 %copy-start.8 = (pred[32,8,128]{2,1,0:T(8,128)(4,1)}, pred[32,8,128]{2,1,0:T(8,128)(4,1)S(1)}, u32[]{:S(2)}) copy-start(pred[32,8,128]{2,1,0:T(8,128)(4,1)S(1)} %get-tuple-element.129) | copy-start | bytes 98308
  77.9 106.5 %copy-start.10 = (pred[32,8,128]{2,1,0:T(8,128)(4,1)}, pred[32,8,128]{2,1,0:T(8,128)(4,1)S(1)}, u32[]{:S(2)}) copy-start(pred[32,8,128]{2,1,0:T(8,128)(4,1)S(1)} %get-tuple-element.131) | copy-start | bytes 98308
  129.6 30.2 %copy-start.28 = (bf16[3,8,128]{2,0,1:T(4,128)(2,1)}, bf16[3,8,128]{2,0,1:T(4,128)(2,1)S(1)}, u32[]{:S(2)}) copy-start(bf16[3,8,128]{2,0,1:T(4,128)(2,1)S(1)} %scatter.49) | copy-start | bytes 18436
  130.8 14.9 %copy-start.15 = (bf16[3,8,128]{2,0,1:T(4,128)(2,1)}, bf16[3,8,128]{2,0,1:T(4,128)(2,1)S(1)}, u32[]{:S(2)}) copy-start(bf16[3,8,128]{2,0,1:T(4,128)(2,1)S(1)} %copy_dynamic-update-slice_fusion.1) | copy-start | bytes 18436
  175.3 3.2 copy-start.2
  184.4 3.0 copy-start.30
  184.4 3.0 copy-start.40
  184.4 3.1 copy-start.38
  184.5 3.4 copy-start.33
  184.5 3.4 copy-start.39
  187.5 28.3 %copy-start.31 = (f32[8,1,8]{2,1,0:T(1,128)}, f32[8,1,8]{2,1,0:T(1,128)S(1)}, u32[]{:S(2)}) copy-start(f32[8,1,8]{2,1,0:T(1,128)S(1)} %fusion.93) | copy-start | bytes 772
  220.9 59.6 %reduce-scatter.13.cloned.1.call-start = ((), (), s32[]{:S(2)}) async-start(), calls=%async_computation.9 | async-start | bytes 294912 | tf_op jit(solution)/shard_map/reduce_scatter | solution.py:171
  232.4 2.9 copy-start.26
  232.4 3.0 copy-start.12
  232.4 30.0 %copy-start.32 = (f32[8,1,8]{2,1,0:T(1,128)S(1)}, f32[8,1,8]{2,1,0:T(1,128)}, u32[]{:S(2)}) copy-start(f32[8,1,8]{2,1,0:T(1,128)} %copy-done.31) | copy-start | bytes 772
  232.4 30.1 %copy-start.34 = (f32[8,128]{1,0:T(8,128)S(1)}, f32[8,128]{1,0:T(8,128)}, u32[]{:S(2)}) copy-start(f32[8,128]{1,0:T(8,128)} %get-tuple-element.119) | copy-start | bytes 12292
  232.5 48.0 %copy-start.29 = (bf16[3,8,128]{2,0,1:T(4,128)(2,1)S(1)}, bf16[3,8,128]{2,0,1:T(4,128)(2,1)}, u32[]{:S(2)}) copy-start(bf16[3,8,128]{2,0,1:T(4,128)(2,1)} %copy-done.28) | copy-start | bytes 18436
  234.5 76.8 %reduce-scatter.17.cloned.1.call-start = ((), (), s32[]{:S(2)}) async-start(), calls=%async_computation.11 | async-start | bytes 294912 | tf_op jit(solution)/shard_map/reduce_scatter | solution.py:171
  235.3 164.7 %all-reduce.9.cloned.1.call-start = ((), (), s32[]{:S(2)}) async-start(), calls=%async_computation.12 | async-start | bytes 786432 | tf_op jit(solution)/shard_map/psum | solution.py:181
  341.1 15.9 %copy-start.16 = (bf16[3,8,128]{2,0,1:T(4,128)(2,1)S(1)}, bf16[3,8,128]{2,0,1:T(4,128)(2,1)}, u32[]{:S(2)}) copy-start(bf16[3,8,128]{2,0,1:T(4,128)(2,1)} %copy-done.15) | copy-start | bytes 18436
  341.1 58.9 %copy-start.7 = (bf16[3,64,512]{2,1,0:T(8,128)(2,1)S(1)}, bf16[3,64,512]{2,1,0:T(8,128)(2,1)}, u32[]{:S(2)}) copy-start(bf16[3,64,512]{2,1,0:T(8,128)(2,1)} %param.22) | copy-start | bytes 589828
  (17 other events, 35.2 us)
Sparse Core Ops, SparseCore 0:
  29.2 28.7 reduce-scatter.6
  60.4 28.5 reduce-scatter.14
  91.3 28.6 reduce-scatter.10
  221.0 28.7 reduce-scatter.8
  252.0 28.4 reduce-scatter.12
  282.7 28.5 reduce-scatter.16
  357.2 42.8 all-reduce.8
where the time goes:
time: 410 us; the launch traced here: 409 us
  blocking collectives  156 us (38%)
  waiting for transfers between devices  131 us (32%)
  local copies, waits for them, and re-layouts  65 us (16%)
  matrix products  29 us (7%)
  between operations  15.8 us (4%)
  other arithmetic  11.9 us (3%)
    reduce_scatter x3, waiting for transfers between devices, body(): lax.psum_scatter(numerator, 'blk', scatter_dimension=0, tiled=True)  46.9 us
    psum x1, waiting for transfers between devices, body(): head_total = lax.psum(partial_value, 'kv')  42.3 us
    all_gather x3, blocking collectives, body(): lax.all_gather(rotated_query.reshape(beams_here, heads_per_group * head_d...  41.9 us
    all_gather x3, blocking collectives, body(): attended = lax.all_gather(own_rows, 'blk', axis=0, tiled=True)  41.9 us
    reduce_scatter x3, waiting for transfers between devices, body(): lax.psum_scatter(jnp.dot(normed, joined_weights, preferred_element_type=j...  41.3 us
    pmax x1, blocking collectives, body(): ceiling = lax.pmax(local_top, 'blk')  27.1 us
    unnamed x1, blocking collectives  27 us
    psum x1, blocking collectives, body(): squares = lax.psum(jnp.sum(stream * stream, axis=1), 'blk')  18.1 us
  transfers between devices with their start and end apart: 7, of which 5 were waited for; matrix products, arithmetic and copies ran while one was open for 16% of the time, Pallas kernels for 0%

commit v1 on v0

v1 whole, which is shorter than its diff:
```python
import math

import jax
import jax.numpy as jnp
from jax import lax
from jax.sharding import PartitionSpec as P

GROUP = 8


NEGATIVE = -1e30
EPSILON = 1e-05
ROPE_BASE = 5000000.0


def rotate(vector, position):
    half_dim = vector.shape[-1] // 2
    exponent = jnp.arange(half_dim, dtype=jnp.float32) * (2.0 / vector.shape[-1])
    frequency = ROPE_BASE ** (-exponent)
    angles = position.astype(jnp.float32)[:, None] * frequency[None, :]
    target_shape = (position.shape[0],) + (1,) * (vector.ndim - 2) + (half_dim,)
    cosines = jnp.cos(angles).reshape(target_shape)
    sine_part = jnp.sin(angles).reshape(target_shape)
    first_half = vector[..., :half_dim]
    second_half = vector[..., half_dim:]
    return jnp.concatenate(
        [
            first_half * cosines - second_half * sine_part,
            second_half * cosines + first_half * sine_part,
        ],
        axis=-1,
    )


def pick(table, index):
    count = table.shape[0]
    hit = index[:, None] == jnp.arange(count, dtype=jnp.int32)[None, :]
    return jnp.sum(jnp.where(hit, table[None, :], 0), axis=1)


def body(
    embeds, attn_gain, w_query, w_key, w_value, w_out, cache_kv, lengths, block_table, parents
):
    parts = lax.axis_size("blk")
    shard = lax.axis_index("blk")
    steps, beams, width_part = embeds.shape
    here = beams // parts
    slots = cache_kv.shape[0]
    block_len, hd = cache_kv.shape[3], cache_kv.shape[4]
    heads = w_query.shape[1] // hd
    groups = beams // GROUP
    width = width_part * parts
    scaling = 1.0 / math.sqrt(hd)
    rows = here * steps
    weights = jnp.concatenate([w_query, w_key, w_value], axis=1)
    all_beams = jnp.arange(beams, dtype=jnp.int32)
    roots, origin = [], []
    for s in range(steps):
        before = roots[-1] if s else all_beams
        roots.append(pick(before, parents[s]))
        origin.append([pick(line, parents[s]) for line in (origin[-1] if s else [])] + [all_beams])
    root = jnp.stack(roots, axis=1)
    position = pick(lengths, root.reshape(-1)).reshape(beams, steps) + jnp.arange(
        steps, dtype=jnp.int32
    )
    slot_ids = shard * slots + jnp.arange(slots, dtype=jnp.int32)
    named = block_table[None] == slot_ids[:, None, None]
    code = jnp.arange(block_table.size, dtype=jnp.int32).reshape(block_table.shape) + 1
    code = jnp.sum(jnp.where(named, code[None], 0), axis=(1, 2)) - 1
    filled = code >= 0
    owner = jnp.where(filled, code // block_table.shape[1], -1)
    logical = code % block_table.shape[1]
    slot_length = jnp.where(filled, pick(lengths, jnp.maximum(owner, 0)) - logical * block_len, 0)
    group_of = jnp.maximum(owner, 0) // GROUP

    stream = embeds.astype(jnp.float32)
    squares = lax.psum(jnp.sum(stream * stream, axis=2), "blk")
    inverse = lax.rsqrt(squares / width + EPSILON)
    normed = (stream * inverse[:, :, None] * attn_gain).astype(jnp.bfloat16)
    normed = normed.transpose(1, 0, 2).reshape(beams * steps, width_part)
    projected = lax.psum_scatter(
        jnp.dot(normed, weights, preferred_element_type=jnp.float32),
        "blk",
        scatter_dimension=0,
        tiled=True,
    )
    own_position = lax.dynamic_slice_in_dim(position, shard * here, here).reshape(rows)
    query = rotate(projected[:, : heads * hd].reshape(rows, heads, hd), own_position).astype(
        jnp.bfloat16
    )
    key = rotate(projected[:, heads * hd : (heads + 1) * hd], own_position).astype(jnp.bfloat16)
    value = projected[:, (heads + 1) * hd :].astype(jnp.bfloat16)
    queries = lax.all_gather(query, "blk", axis=0, tiled=True)
    by_group = queries.reshape(groups, GROUP * steps * heads, hd)
    scores = (
        jnp.einsum(
            "sqd,skd->sqk", by_group[group_of], cache_kv[:, 0, 0], preferred_element_type=jnp.float32
        )
        * scaling
    ).reshape(slots, GROUP * steps, heads, block_len)
    root_by_group = root.reshape(groups, GROUP * steps)[group_of]
    active = (
        (root_by_group == owner[:, None])[:, :, None, None]
        & (jnp.arange(block_len, dtype=jnp.int32) < slot_length[:, None])[:, None, None, :]
    )
    slot_top = jnp.max(jnp.where(active, scores, NEGATIVE), axis=-1)
    in_group = (group_of[:, None] == jnp.arange(groups, dtype=jnp.int32)) & filled[:, None]
    group_top = jnp.max(
        jnp.where(in_group[:, :, None, None], slot_top[:, None], NEGATIVE), axis=0
    ).reshape(beams * steps, heads)
    step_of = jnp.arange(rows, dtype=jnp.int32) % steps
    own_origin = jnp.stack(
        [
            jnp.stack([origin[s][u] if u <= s else all_beams * 0 - 1 for u in range(steps)], axis=1)
            for s in range(steps)
        ],
        axis=1,
    )
    own_origin = lax.dynamic_slice_in_dim(own_origin, shard * here, here).reshape(rows, steps)
    beam_of = shard * here + jnp.arange(rows, dtype=jnp.int32) // steps
    linked = jnp.zeros((rows, rows), bool)
    for u in range(steps):
        linked |= (own_origin[:, u : u + 1] == beam_of[None, :]) & (step_of == u)[None, :]
    new_scores = jnp.where(
        linked[:, None, :],
        jnp.einsum("rhd,kd->rhk", query, key, preferred_element_type=jnp.float32) * scaling,
        NEGATIVE,
    )
    own_top = jnp.maximum(
        lax.dynamic_slice_in_dim(group_top, shard * rows, rows), jnp.max(new_scores, axis=-1)
    )
    ceiling = lax.pmax(
        lax.dynamic_update_slice_in_dim(group_top, own_top, shard * rows, 0), "blk"
    )
    slot_ceiling = ceiling.reshape(groups, GROUP * steps, heads)[group_of]
    probs = jnp.exp(jnp.where(active, scores - slot_ceiling[..., None], NEGATIVE))
    slot_denominator = jnp.sum(probs, axis=-1)
    slot_numerator = jnp.einsum(
        "srhk,skd->srhd",
        probs.astype(jnp.bfloat16),
        cache_kv[:, 0, 1],
        preferred_element_type=jnp.float32,
    )
    joined = jnp.concatenate(
        [slot_numerator.reshape(slots, -1), slot_denominator.reshape(slots, -1)], axis=1
    )
    joined = jnp.einsum(
        "sg,sx->gx", in_group.astype(jnp.float32), joined, precision=lax.Precision.HIGHEST
    )
    cut = GROUP * steps * heads * hd
    numerator = lax.psum_scatter(
        joined[:, :cut].reshape(beams * steps, heads, hd), "blk", scatter_dimension=0, tiled=True
    )
    denominator = lax.psum_scatter(
        joined[:, cut:].reshape(beams * steps, heads), "blk", scatter_dimension=0, tiled=True
    )
    own_ceiling = lax.dynamic_slice_in_dim(ceiling, shard * rows, rows)
    new_probs = jnp.exp(new_scores - own_ceiling[..., None])
    numerator += jnp.einsum(
        "rhk,kd->rhd", new_probs.astype(jnp.bfloat16), value, preferred_element_type=jnp.float32
    )
    denominator += jnp.sum(new_probs, axis=-1)
    attended = (numerator / denominator[..., None]).astype(jnp.bfloat16).reshape(rows, heads * hd)
    attended = lax.all_gather(attended, "blk", axis=0, tiled=True)
    partial = jnp.dot(attended, w_out, preferred_element_type=jnp.float32)
    total = lax.psum(partial, "kv").reshape(beams, steps, width_part).transpose(1, 0, 2)
    out = (stream + total).astype(jnp.bfloat16)
    last = own_origin.reshape(here, steps, steps)[:, -1]
    chosen = (
        (last[:, :, None] == beam_of) & (jnp.arange(steps)[None, :, None] == step_of)
    ).astype(jnp.bfloat16)
    appended = jnp.einsum(
        "bur,rcd->ubcd",
        chosen,
        jnp.stack([key, value], axis=1),
        preferred_element_type=jnp.float32,
    ).astype(jnp.bfloat16)
    return out, appended[:, :, None]


def solution(mesh):
    return jax.shard_map(
        body,
        mesh=mesh,
        in_specs=(
            P(None, None, "blk"),
            P("blk"),
            P("blk", "kv"),
            P("blk", "kv"),
            P("blk", "kv"),
            P("kv", "blk"),
            P("blk", "kv", None, None, None),
            P(),
            P(),
            P(),
        ),
        out_specs=(P(None, None, "blk"), P(None, "blk", "kv", None, None)),
        check_vma=False,
    )
```

time: 410 us -> 256 us (0.62)
  blocking collectives: 156 us -> 74.2 us
  local copies, waits for them, and re-layouts: 65 us -> 13.6 us
  matrix products: 29 us -> 13.6 us
    all_gather x6 -> x2, blocking collectives: 83.8 us -> 28.9 us  [the longest x1 14.5 us: body(): queries = lax.all_gather(query, 'blk', axis=0, tiled=True)]
    scatter x8 -> x0, local copies, waits for them, and re-layouts: 31.2 us -> none  [the longest x1 15.5 us: body(): jnp.zeros((total_slots + 1,), jnp.int32).at[flat_table]]
    reduce_scatter x6 -> x2, waiting for transfers between devices: 88.2 us -> 57.7 us  [the longest x1 31.2 us: body(): lax.psum_scatter(joined[:, :cut].reshape(beams * steps, heads, hd), 'blk'...]
    unnamed x7 -> x5, waiting for transfers between devices: 0.12 us -> 27.3 us
    unnamed x1 -> x0, blocking collectives: 27 us -> none
    gather x27 -> x5, local copies, waits for them, and re-layouts: 21.8 us -> 3.71 us  [the longest x3 2.28 us: body(): slot_ceiling = ceiling.reshape(groups, GROUP * steps, heads)[group_of]]
    dot_general x23 -> x8, matrix products: 29 us -> 13.6 us  [the longest x1 4.08 us: body(): jnp.einsum('sqd,skd->sqk', by_group[group_of], cache_kv[:, 0, 0], preferr...]
  transfers between devices with their start and end apart: 7 -> 4, of which waited for: 5 -> 4; matrix products, arithmetic and copies ran while one was open for 16% -> 3% of each run, Pallas kernels for 0% -> 0%
where the time goes in v1:
time: 256 us; the launch traced here: 255 us
  waiting for transfers between devices  127 us (50%)
  blocking collectives  74.2 us (29%)
  between operations  14.2 us (6%)
  local copies, waits for them, and re-layouts  13.6 us (5%)
  matrix products  13.6 us (5%)
  other arithmetic  12 us (5%)
    psum x1, waiting for transfers between devices, body(): lax.psum(partial, 'kv').reshape(beams, steps, width_part).transpose(1, 0, 2)  42.3 us
    reduce_scatter x1, waiting for transfers between devices, body(): lax.psum_scatter(joined[:, :cut].reshape(beams * steps, heads, hd), 'blk'...  31.2 us
    unnamed x5, waiting for transfers between devices  27.3 us
    pmax x1, blocking collectives, body(): lax.pmax(lax.dynamic_update_slice_in_dim(group_top, own_top, shard * rows...  27.2 us
    reduce_scatter x1, waiting for transfers between devices, body(): lax.psum_scatter(jnp.dot(normed, weights, preferred_element_type=jnp.floa...  26.4 us
    psum x1, blocking collectives, body(): squares = lax.psum(jnp.sum(stream * stream, axis=2), 'blk')  18.1 us
    all_gather x1, blocking collectives, body(): queries = lax.all_gather(query, 'blk', axis=0, tiled=True)  14.5 us
    all_gather x1, blocking collectives, body(): attended = lax.all_gather(attended, 'blk', axis=0, tiled=True)  14.5 us
  transfers between devices with their start and end apart: 4, of which 4 were waited for; matrix products, arithmetic and copies ran while one was open for 3% of the time, Pallas kernels for 0%

profile of v1, /device:TPU:0, one launch (start us, length us, event | category | flops | bytes accessed | tf_op | source)
XLA Modules:
  0.0 255.0 jit_solution(4008387594843132540)
XLA Ops:
  7.2 1.2 fusion.31
  8.6 18.1 %psum.14 = f32[3,64]{1,0:T(4,128)S(1)} all-reduce(f32[3,64]{1,0:T(4,128)S(1)} %copy.101), channel_id=1, replica_groups=mesh['kv'=4,'blk'=8] {'blk'}, use_global_device_ids=true, to_apply=%region_6.7 | all-reduce | flops 192 | bytes 1536 | tf_op jit(solution)/shard_map/psum | solution.py:77
  26.8 1.2 fusion.35
  28.1 2.8 %fusion.16 = f32[192,1280]{1,0:T(8,128)} fusion(bf16[192,512]{1,0:T(8,128)(2,1)S(1)} %reshape.565, bf16[512,128]{1,0:T(8,128)(2,1)} %param.14, bf16[512,128]{1,0:T(8,128)(2,1)} %param.13, bf16[512,1024]{1,0:T(8,128)(2,1)} %param.12), kind=kOutput, calls=%fused_computation.22 | convolution fusion | flops 255590400 | bytes 2490368 | tf_op jit(solution)/shard_map/dot_general | solution.py:82
  31.0 0.8 select_reduce_fusion
  34.8 26.4 %reduce-scatter.6.cloned.1.call-done = f32[24,1280]{1,0:T(8,128)} async-done(((f32[192,1280]{1,0:T(8,128)}), f32[24,1280]{1,0:T(8,128)}) %reduce-scatter.6.cloned.1.call-update) | async-done | bytes 122896 | tf_op jit(solution)/shard_map/reduce_scatter | solution.py:81
  61.2 0.9 slice_bitcast_fusion
  62.2 0.9 subtract_convert_fusion.1
  63.3 14.5 %all_gather.6 = bf16[192,8,128]{2,1,0:T(8,128)(2,1)S(1)} all-gather(bf16[24,8,128]{2,1,0:T(8,128)(2,1)S(1)} %pad_maximum_fusion), channel_id=1, replica_groups=mesh['kv'=4,'blk'=8] {'blk'}, dimensions={0}, use_global_device_ids=true | all-gather | bytes 442368 | tf_op jit(solution)/shard_map/all_gather | solution.py:93
  77.8 0.8 gather_fusion.1
  78.6 4.1 %fusion.4 = (f32[32,192]{1,0:T(8,128)S(1)}, f32[32,192,128]{2,1,0:T(8,128)}) fusion(pred[32,24,128]{2,1,0:T(8,128)(4,1)S(1)} %broadcast_and_fusion, bf16[32,192,128]{2,1,0:T(8,128)(2,1)S(1)} %gather_fusion.1, bf16[32,1,2,128,128]{4,3,2,1,0:T(8,128)(2,1)} %param.16), kind=kOutput, calls=%fused_computation.9 | convolution fusion | flops 203679744 | bytes 5890048 | tf_op jit(solution)/shard_map/sqd,skd->sqk/dot_general | solution.py:96
  83.1 0.9 fusion.70
  83.9 27.2 %pmax.7 = f32[192,8]{1,0:T(8,128)S(1)} all-reduce(f32[192,8]{1,0:T(8,128)S(1)} %maximum_dynamic-update-slice_fusion), channel_id=1, replica_groups=mesh['kv'=4,'blk'=8] {'blk'}, use_global_device_ids=true, to_apply=%region_15.16 | all-reduce | flops 1536 | bytes 12288 | tf_op jit(solution)/shard_map/pmax | solution.py:132
  111.8 0.7 copy.111
  112.6 0.9 copy.109
  113.5 1.0 copy.112
  114.5 3.7 %fusion.6 = f32[32,192]{1,0:T(8,128)S(1)} fusion(f32[32,192,128]{2,1,0:T(8,128)} %get-tuple-element.38, f32[32,192]{1,0:T(8,128)S(1)} %copy.112, pred[32,24,128]{2,1,0:T(8,128)(4,1)S(1)} %broadcast_and_fusion), kind=kLoop, calls=%fused_computation.11 | loop fusion | flops 3139584 | bytes 3293184 | tf_op jit(solution)/shard_map/reduce_sum | solution.py:137
  118.2 3.1 %fusion.10 = f32[32,24,8,128]{3,2,1,0:T(8,128)S(1)} fusion(f32[32,192,128]{2,1,0:T(8,128)S(1)} %copy-done.1, f32[32,24,8]{2,1,0:T(8,128)} %copy.109, pred[32,24,128]{2,1,0:T(8,128)(4,1)S(1)} %broadcast_and_fusion, bf16[32,1,2,128,128]{4,3,2,1,0:T(8,128)(2,1)S(1)} %copy-done.2), kind=kOutput, calls=%fused_computation.17 | convolution fusion | flops 204472320 | bytes 7462912 | tf_op jit(solution)/shard_map/srhk,skd->srhd/dot_general | solution.py:138
  121.3 1.8 copy.129
  123.1 1.2 fusion
  124.3 0.7 reshape.575
  125.2 1.0 reshape.574
  126.5 27.2 %reduce-scatter.10.cloned.1.call-done = f32[24,8]{1,0:T(8,128)} async-done(((f32[192,8]{1,0:T(8,128)}), f32[24,8]{1,0:T(8,128)}) %reduce-scatter.10.cloned.1.call-update) | async-done | bytes 784
  153.7 0.7 add.214
  154.4 31.2 %reduce-scatter.8.cloned.1.call-done = f32[24,8,128]{2,1,0:T(8,128)} async-done(((f32[192,8,128]{2,1,0:T(8,128)}), f32[24,8,128]{2,1,0:T(8,128)}) %reduce-scatter.8.cloned.1.call-update) | async-done | bytes 98320 | tf_op jit(solution)/shard_map/reduce_scatter | solution.py:151
  185.6 1.1 fusion.24
  186.8 14.5 %all_gather.7 = bf16[192,1024]{1,0:T(8,128)(2,1)S(1)} all-gather(bf16[24,1024]{1,0:T(8,128)(2,1)S(1)} %bitcast.132), channel_id=1, replica_groups=mesh['kv'=4,'blk'=8] {'blk'}, dimensions={0}, use_global_device_ids=true | all-gather | bytes 442368 | tf_op jit(solution)/shard_map/all_gather | solution.py:164
  201.6 1.0 reshape.577
  202.6 0.7 fusion.55
  204.1 42.3 %all-reduce.3.cloned.1.call-done = f32[3,64,512]{2,0,1:T(4,128)} async-done(((f32[3,64,512]{2,0,1:T(4,128)}), f32[3,64,512]{2,0,1:T(4,128)}) %all-reduce.3.cloned.1.call-update) | async-done | bytes 393232 | tf_op jit(solution)/shard_map/psum | solution.py:166
  246.5 1.3 fusion.34
  247.7 0.7 copy.113
  (87 shorter events, 6.3 us)
Async XLA Ops:
  7.2 194.1 %copy-start = (bf16[1024,512]{1,0:T(8,128)(2,1)S(1)}, bf16[1024,512]{1,0:T(8,128)(2,1)}, u32[]{:S(2)}) copy-start(bf16[1024,512]{1,0:T(8,128)(2,1)} %param.15) | copy-start | bytes 3145732
  7.2 23.8 %copy-start.5 = (s32[64,64]{1,0:T(8,128)S(1)}, s32[64,64]{1,0:T(8,128)}, u32[]{:S(2)}) copy-start(s32[64,64]{1,0:T(8,128)} %param.18) | copy-start | bytes 49156
  7.2 24.7 %copy-start.7 = (s32[3,64]{1,0:T(4,128)S(1)}, s32[3,64]{1,0:T(4,128)}, u32[]{:S(2)}) copy-start(s32[3,64]{1,0:T(4,128)} %param.19) | copy-start | bytes 2308
  7.2 54.0 %reduce-scatter.6.cloned.1.call-start = ((), (), s32[]{:S(2)}) async-start(), calls=%async_computation.3 | async-start | bytes 1105920 | tf_op jit(solution)/shard_map/reduce_scatter | solution.py:81
  8.5 24.3 %copy-start.8 = (s32[64]{0:T(128)S(1)}, s32[64]{0:T(128)}, u32[]{:S(2)}) copy-start(s32[64]{0:T(128)} %param.17) | copy-start | bytes 772
  8.5 24.7 %copy-start.6 = (s32[64,1,3]{0,2,1:T(4,128)S(1)}, s32[64,1,3]{0,2,1:T(4,128)}, u32[]{:S(2)}) copy-start(s32[64,1,3]{0,2,1:T(4,128)} %constant.105.clone.1) | copy-start | bytes 2308
  30.9 122.8 %reduce-scatter.10.cloned.1.call-start = ((), (), s32[]{:S(2)}) async-start(), calls=%async_computation.6 | async-start | bytes 110592
  82.7 35.5 %copy-start.2 = (bf16[32,1,2,128,128]{4,3,2,1,0:T(8,128)(2,1)S(1)}, bf16[32,1,2,128,128]{4,3,2,1,0:T(8,128)(2,1)}, u32[]{:S(2)}) copy-start(bf16[32,1,2,128,128]{4,3,2,1,0:T(8,128)(2,1)} %param.16) | copy-start | bytes 6291460
  114.5 3.7 %copy-start.1 = (f32[32,192,128]{2,1,0:T(8,128)S(1)}, f32[32,192,128]{2,1,0:T(8,128)}, u32[]{:S(2)}) copy-start(f32[32,192,128]{2,1,0:T(8,128)} %get-tuple-element.38) | copy-start | bytes 9437188
  123.1 3.2 %copy-start.4 = (f32[24,8,24]{2,1,0:T(8,128)S(1)}, f32[24,8,24]{2,1,0:T(8,128)}, u32[]{:S(2)}) copy-start(f32[24,8,24]{2,1,0:T(8,128)} %get-tuple-element.40) | copy-start | bytes 55300
  125.0 60.6 %reduce-scatter.8.cloned.1.call-start = ((), (), s32[]{:S(2)}) async-start(), calls=%async_computation.4 | async-start | bytes 884736 | tf_op jit(solution)/shard_map/reduce_scatter | solution.py:151
  125.2 121.3 %copy-start.3 = (bf16[3,64,512]{2,1,0:T(8,128)(2,1)S(1)}, bf16[3,64,512]{2,1,0:T(8,128)(2,1)}, u32[]{:S(2)}) copy-start(bf16[3,64,512]{2,1,0:T(8,128)(2,1)} %param.10) | copy-start | bytes 589828
  126.2 120.3 %all-reduce.3.cloned.1.call-start = ((), (), s32[]{:S(2)}) async-start(), calls=%async_computation.5 | async-start | bytes 1048576 | tf_op jit(solution)/shard_map/psum | solution.py:166
Sparse Core Ops, SparseCore 0:
  31.0 30.1 reduce-scatter.5
  125.2 28.4 reduce-scatter.9
  156.0 29.6 reduce-scatter.7
  202.7 43.6 all-reduce.2

commit v2 on v1

v2 whole, which is shorter than its diff:
```python
import functools
import math

import jax
import jax.numpy as jnp
from jax import lax
from jax.experimental import pallas as pl
from jax.experimental.pallas import tpu as pltpu
from jax.sharding import PartitionSpec as P

GROUP = 8


NEGATIVE = -1e30
EPSILON = 1e-05
ROPE_BASE = 5000000.0


MESH = pl.DeviceIdType.MESH


def remote(source, target, send, recv, axis, index):
    return pltpu.make_async_remote_copy(
        src_ref=source,
        dst_ref=target,
        send_sem=send,
        recv_sem=recv,
        device_id={axis: index},
        device_id_type=MESH,
    )


def kernel(
    sizes,
    slot_ref,
    last_ref,
    embeds_ref,
    gain_ref,
    root_ref,
    cos_ref,
    sin_ref,
    linked_ref,
    chosen_ref,
    wq_hbm,
    wk_hbm,
    wv_hbm,
    wo_hbm,
    cache_hbm,
    out_ref,
    appended_ref,
    weights,
    w_out,
    cache,
    stream,
    squares,
    part,
    sib_part,
    z_part,
    q_all,
    scores,
    seg_top,
    tops,
    ceilings,
    seg_num,
    seg_den,
    num,
    den,
    sib_num,
    sib_den,
    z_num,
    z_den,
    att_all,
    out_part,
    kv_part,
    out_rows,
    load_sem,
    sq_send,
    sq_recv,
    sib_send,
    sib_recv,
    z_send,
    z_recv,
    q_send,
    q_recv,
    top_send,
    top_recv,
    nsib_send,
    nsib_recv,
    nz_send,
    nz_recv,
    a_send,
    a_recv,
    kv_send,
    kv_recv,
    o_send,
    o_recv,
):
    n, kvn, steps, here, heads, hd, slots, width = sizes
    me = lax.axis_index("blk")
    kv = lax.axis_index("kv")
    chips = n // 2
    chip, core = me // 2, lax.rem(me, 2)
    sibling = me + 1 - 2 * core
    rows = steps * here
    beams = n * here
    quarter = n * rows // kvn
    lanes = heads * rows
    scaling = 1.0 / math.sqrt(hd)
    wide = w_out.shape[1]

    barrier = pltpu.get_barrier_semaphore()
    for d in range(1, n):
        pl.semaphore_signal(
            barrier, inc=1, device_id={"blk": lax.rem(me + d, n)}, device_id_type=MESH
        )
    for d in range(1, kvn):
        pl.semaphore_signal(
            barrier, inc=1, device_id={"kv": lax.rem(kv + d, kvn)}, device_id_type=MESH
        )
    qw = heads * hd
    loads = [
        pltpu.make_async_copy(wq_hbm, weights.at[:, pl.ds(0, qw)], load_sem.at[0]),
        pltpu.make_async_copy(wk_hbm, weights.at[:, pl.ds(qw, hd)], load_sem.at[1]),
        pltpu.make_async_copy(wv_hbm, weights.at[:, pl.ds(qw + hd, hd)], load_sem.at[2]),
        pltpu.make_async_copy(cache_hbm, cache, load_sem.at[3]),
        pltpu.make_async_copy(wo_hbm, w_out, load_sem.at[4]),
    ]
    for load in loads:
        load.start()

    x = embeds_ref[...].astype(jnp.float32)
    eye = lax.broadcasted_iota(jnp.int32, (beams, beams), 0) == lax.broadcasted_iota(
        jnp.int32, (beams, beams), 1
    )
    for s in range(steps):
        column = jnp.sum(x[s] * x[s], axis=1, keepdims=True)
        squares[0, s : s + 1, 0:beams] = jnp.sum(jnp.where(eye, column, 0.0), axis=0, keepdims=True)
    pl.semaphore_wait(barrier, n - 1 + kvn - 1)
    sends = []
    for d in range(1, n):
        sends.append(
            remote(
                squares.at[0], squares.at[d], sq_send.at[d], sq_recv.at[d], "blk", lax.rem(me + d, n)
            )
        )
        sends[-1].start()
    by_part = x.reshape(steps, n, here, wide).transpose(1, 0, 2, 3).reshape(n * rows, wide)
    stream[...] = by_part
    for send in sends:
        send.wait()
    normed = []
    for s in range(steps):
        total = squares[0, s : s + 1, 0:beams]
        for d in range(1, n):
            total = total + squares[d, s : s + 1, 0:beams]
        column = jnp.sum(jnp.where(eye, total, 0.0), axis=1, keepdims=True)
        normed.append(x[s] * lax.rsqrt(column / width + EPSILON) * gain_ref[...])
    normed = (
        jnp.stack(normed)
        .reshape(steps, chips, 2, here, wide)
        .transpose(2, 1, 0, 3, 4)
        .reshape(2, chips * rows, wide)
        .astype(jnp.bfloat16)
    )
    for load in loads[:3]:
        load.wait()
    for c in range(2):
        part[c] = jnp.dot(
            normed[c], weights[...], preferred_element_type=jnp.float32
        ).reshape(sib_part.shape)
    over = remote(part.at[1 - core], sib_part, sib_send, sib_recv, "blk", sibling)
    over.start()
    over.wait()
    sib_part[...] = part[core] + sib_part[...]
    sends = []
    for d in range(1, chips):
        t = lax.rem(chip + d, chips)
        sends.append(
            remote(
                sib_part.at[t], z_part.at[d], z_send.at[d], z_recv.at[d], "blk", 2 * t + core
            )
        )
        sends[-1].start()
    for send in sends:
        send.wait()
    total = sib_part[chip]
    for d in range(1, chips):
        total = total + z_part[d]

    cos, sin = cos_ref[...], sin_ref[...]

    def rope(block):
        return block * cos + pltpu.roll(block, hd // 2, 1) * sin

    query = jnp.concatenate(
        [rope(total[:, h * hd : (h + 1) * hd]) for h in range(heads)], axis=0
    ).astype(jnp.bfloat16)
    key = rope(total[:, qw : qw + hd]).astype(jnp.bfloat16)
    value = total[:, qw + hd :].astype(jnp.bfloat16)

    def gather(ref, send_sem, recv_sem):
        first = []
        for d in range(1, chips):
            first.append(
                remote(
                    ref.at[me],
                    ref.at[me],
                    send_sem.at[d],
                    recv_sem.at[d],
                    "blk",
                    2 * lax.rem(chip + d, chips) + core,
                )
            )
            first[-1].start()
        second = [remote(ref.at[me], ref.at[me], send_sem.at[0], recv_sem.at[0], "blk", sibling)]
        second[0].start()
        for d in range(1, chips):
            first[d - 1].wait_recv()
            origin = 2 * lax.rem(chip + chips - d, chips) + core
            second.append(
                remote(
                    ref.at[origin],
                    ref.at[origin],
                    send_sem.at[chips + d],
                    recv_sem.at[chips + d],
                    "blk",
                    sibling,
                )
            )
            second[-1].start()
        for copy in second:
            copy.wait()
        for copy in first:
            copy.wait_send()

    q_all[me] = query
    gather(q_all, q_send, q_recv)

    contract_last = (((1,), (1,)), ((), ()))
    contract_first = (((0,), (0,)), ((), ()))
    own_scores = jnp.where(
        linked_ref[...] > 0,
        lax.dot_general(key, query, contract_last, preferred_element_type=jnp.float32) * scaling,
        NEGATIVE,
    )
    own_top = jnp.max(own_scores, axis=0, keepdims=True)
    appended_ref[...] = jnp.dot(
        chosen_ref[...],
        jnp.concatenate([key, value], axis=1),
        preferred_element_type=jnp.float32,
    ).astype(jnp.bfloat16)
    loads[3].wait()
    block = cache.shape[2]
    token = lax.broadcasted_iota(jnp.int32, (block, lanes), 0)

    def look(i, top):
        group = slot_ref[1, i]
        score = (
            lax.dot_general(
                cache[slot_ref[0, i], 0],
                q_all[group],
                contract_last,
                preferred_element_type=jnp.float32,
            )
            * scaling
        )
        active = (root_ref[group] == slot_ref[2, i]) & (token < slot_ref[3, i])
        score = jnp.where(active, score, NEGATIVE)
        scores[i] = score
        kept = jnp.where(slot_ref[4, i] > 0, top, NEGATIVE)
        top = jnp.maximum(kept, jnp.max(score, axis=0, keepdims=True))
        seg_top[i] = top
        return top

    lax.fori_loop(0, slots, look, jnp.full((1, lanes), NEGATIVE, jnp.float32), unroll=4)
    for g in range(n):
        top = jnp.where(last_ref[1, g] > 0, seg_top[last_ref[0, g]], NEGATIVE)
        tops[0, g : g + 1, :] = jnp.where(me == g, jnp.maximum(top, own_top), top)
    sends = []
    for d in range(1, n):
        sends.append(
            remote(tops.at[0], tops.at[d], top_send.at[d], top_recv.at[d], "blk", lax.rem(me + d, n))
        )
        sends[-1].start()
    for send in sends:
        send.wait()
    ceiling = tops[0]
    for d in range(1, n):
        ceiling = jnp.maximum(ceiling, tops[d])
    ceilings[...] = ceiling[:, None, :]

    def add(i, carry):
        total, count = carry
        probs = jnp.exp(scores[i] - ceilings[slot_ref[1, i]])
        same = slot_ref[4, i] > 0
        count = jnp.where(same, count, 0.0) + jnp.sum(probs, axis=0, keepdims=True)
        total = jnp.where(same, total, 0.0) + lax.dot_general(
            probs.astype(jnp.bfloat16),
            cache[slot_ref[0, i], 1],
            contract_first,
            preferred_element_type=jnp.float32,
        )
        seg_num[i] = total
        seg_den[i] = count
        return total, count

    lax.fori_loop(
        0,
        slots,
        add,
        (jnp.zeros((lanes, hd), jnp.float32), jnp.zeros((1, lanes), jnp.float32)),
        unroll=2,
    )
    own_probs = jnp.exp(own_scores - ceilings[me])
    own_num = lax.dot_general(
        own_probs.astype(jnp.bfloat16), value, contract_first, preferred_element_type=jnp.float32
    )
    own_den = jnp.sum(own_probs, axis=0, keepdims=True)
    for t in range(chips):
        for c in range(2):
            g = 2 * t + c
            some = last_ref[1, g] > 0
            num[c, t] = jnp.where(some, seg_num[last_ref[0, g]], 0.0)
            den[c, t] = jnp.where(some, seg_den[last_ref[0, g]], 0.0)
    pair = [
        remote(num.at[1 - core], sib_num, nsib_send.at[0], nsib_recv.at[0], "blk", sibling),
        remote(den.at[1 - core], sib_den, nsib_send.at[1], nsib_recv.at[1], "blk", sibling),
    ]
    for copy in pair:
        copy.start()
    for copy in pair:
        copy.wait()
    sib_num[...] = sib_num[...] + num[core]
    sib_den[...] = sib_den[...] + den[core]
    sends = []
    for d in range(1, chips):
        t = lax.rem(chip + d, chips)
        for k, (source, target) in enumerate(((sib_num, z_num), (sib_den, z_den))):
            sends.append(
                remote(
                    source.at[t],
                    target.at[d],
                    nz_send.at[k, d],
                    nz_recv.at[k, d],
                    "blk",
                    2 * t + core,
                )
            )
            sends[-1].start()
    numerator = own_num + sib_num[chip]
    denominator = own_den + sib_den[chip]
    for send in sends:
        send.wait()
    for d in range(1, chips):
        numerator = numerator + z_num[d]
        denominator = denominator + z_den[d]
    turn = lax.broadcasted_iota(jnp.int32, (lanes, lanes), 0) == lax.broadcasted_iota(
        jnp.int32, (lanes, lanes), 1
    )
    column = jnp.sum(jnp.where(turn, denominator, 0.0), axis=1, keepdims=True)
    att_all[me] = (numerator / column).astype(jnp.bfloat16)
    gather(att_all, a_send, a_recv)

    attended = att_all[...].astype(jnp.float32).reshape(n, heads, rows, hd)
    attended = jnp.concatenate(
        [attended[:, h].reshape(n * rows, hd) for h in range(heads)], axis=1
    ).astype(jnp.bfloat16)
    loads[4].wait()
    out_part[...] = jnp.dot(
        attended, w_out[...], preferred_element_type=jnp.float32
    ).reshape(out_part.shape)
    sends = []
    for d in range(1, kvn):
        t = lax.rem(kv + d, kvn)
        sends.append(
            remote(out_part.at[t], kv_part.at[d], kv_send.at[d], kv_recv.at[d], "kv", t)
        )
        sends[-1].start()
    total = out_part[kv]
    for send in sends:
        send.wait()
    for d in range(1, kvn):
        total = total + kv_part[d]
    start = pl.multiple_of(kv * quarter, 16)
    out_rows[kv] = (stream[pl.ds(start, quarter)] + total).astype(jnp.bfloat16)
    sends = []
    for d in range(1, kvn):
        t = lax.rem(kv + d, kvn)
        sends.append(
            remote(out_rows.at[kv], out_rows.at[kv], o_send.at[d], o_recv.at[d], "kv", t)
        )
        sends[-1].start()
    for send in sends:
        send.wait()
    result = out_rows[...].astype(jnp.float32).reshape(n, steps, here, wide)
    out_ref[...] = result.transpose(1, 0, 2, 3).reshape(steps, beams, wide).astype(jnp.bfloat16)


def pick(table, index):
    count = table.shape[0]
    hit = index[:, None] == jnp.arange(count, dtype=jnp.int32)[None, :]
    return jnp.sum(jnp.where(hit, table[None, :], 0), axis=1)


def body(
    embeds, attn_gain, w_query, w_key, w_value, w_out, cache_kv, lengths, block_table, parents
):
    n = lax.axis_size("blk")
    kvn = lax.axis_size("kv")
    shard = lax.axis_index("blk")
    steps, beams, wide = embeds.shape
    here = beams // n
    slots = cache_kv.shape[0]
    block, hd = cache_kv.shape[3], cache_kv.shape[4]
    heads = w_query.shape[1] // hd
    rows = here * steps
    lanes = heads * rows
    all_beams = jnp.arange(beams, dtype=jnp.int32)
    roots, origin = [], []
    for s in range(steps):
        before = roots[-1] if s else all_beams
        roots.append(pick(before, parents[s]))
        origin.append([pick(line, parents[s]) for line in (origin[-1] if s else [])] + [all_beams])
    root = jnp.stack(roots)
    slot_ids = shard * slots + jnp.arange(slots, dtype=jnp.int32)
    named = block_table[None] == slot_ids[:, None, None]
    code = jnp.arange(block_table.size, dtype=jnp.int32).reshape(block_table.shape) + 1
    code = jnp.sum(jnp.where(named, code[None], 0), axis=(1, 2)) - 1
    filled = code >= 0
    owner = jnp.where(filled, code // block_table.shape[1], -1)
    logical = code % block_table.shape[1]
    tokens = jnp.where(filled, pick(lengths, jnp.maximum(owner, 0)) - logical * block, 0)
    group = jnp.where(filled, owner // GROUP, n - 1)
    place = jnp.arange(slots, dtype=jnp.int32)
    rank = jnp.sum(
        (group[None, :] < group[:, None])
        | ((group[None, :] == group[:, None]) & (place[None, :] < place[:, None])),
        axis=1,
    )
    table = jnp.stack([place, group, owner, tokens])
    table = jnp.sum(jnp.where((rank[:, None] == place[None, :])[None], table[:, :, None], 0), axis=1)
    same = jnp.concatenate(
        [jnp.zeros((1,), jnp.int32), (table[1, 1:] == table[1, :-1]).astype(jnp.int32)]
    )
    table = jnp.concatenate([table, same[None]])
    upto = jnp.sum(group[None, :] <= jnp.arange(n, dtype=jnp.int32)[:, None], axis=1)
    held = jnp.sum(group[None, :] == jnp.arange(n, dtype=jnp.int32)[:, None], axis=1)
    last = jnp.stack([jnp.maximum(upto - 1, 0), held]).astype(jnp.int32)

    root_rows = root.reshape(steps, n, here).transpose(1, 0, 2).reshape(n, 1, 1, rows)
    root_rows = jnp.broadcast_to(root_rows, (n, 1, heads, rows)).reshape(n, 1, lanes)
    own = lax.dynamic_slice_in_dim(root, shard * here, here, 1)
    position = pick(lengths, own.reshape(-1)).reshape(steps, here) + jnp.arange(
        steps, dtype=jnp.int32
    )[:, None]
    exponent = jnp.arange(hd // 2, dtype=jnp.float32) * (2.0 / hd)
    angles = position.reshape(rows).astype(jnp.float32)[:, None] * (ROPE_BASE ** (-exponent))
    cos, sin = jnp.cos(angles), jnp.sin(angles)
    cos = jnp.concatenate([cos, cos], axis=1)
    sin = jnp.concatenate([-sin, sin], axis=1)
    origin_own = jnp.stack(
        [
            jnp.stack([origin[s][u] if u <= s else all_beams * 0 - 1 for u in range(steps)])
            for s in range(steps)
        ]
    )
    origin_own = lax.dynamic_slice_in_dim(origin_own, shard * here, here, 2) - shard * here
    seat = jnp.arange(here, dtype=jnp.int32)
    meets = origin_own.transpose(0, 2, 1)[:, :, :, None] == seat
    linked = meets.transpose(2, 3, 0, 1).reshape(rows, 1, rows)
    linked = jnp.broadcast_to(linked, (rows, heads, rows)).reshape(rows, lanes).astype(jnp.float32)
    chosen = meets[-1].transpose(1, 0, 2)[:, :, None, :] & (
        jnp.arange(steps)[:, None, None, None] == jnp.arange(steps)[None, None, :, None]
    )
    chosen = chosen.reshape(rows, rows).astype(jnp.bfloat16)

    chips = n // 2
    total_rows = n * rows
    columns = (heads + 2) * hd
    quarter = total_rows // kvn
    sizes = (n, kvn, steps, here, heads, hd, slots, wide * n)
    bf16, f32 = jnp.bfloat16, jnp.float32
    dma = pltpu.SemaphoreType.DMA
    lane_room = -(-beams // 128) * 128
    vmem = pl.BlockSpec(memory_space=pltpu.VMEM)
    smem = pl.BlockSpec(memory_space=pltpu.SMEM)
    hbm = pl.BlockSpec(memory_space=pl.ANY)
    out, appended = pl.pallas_call(
        functools.partial(kernel, sizes),
        out_shape=(
            jax.ShapeDtypeStruct((steps, beams, wide), bf16),
            jax.ShapeDtypeStruct((rows, 2 * hd), bf16),
        ),
        in_specs=[smem, smem] + [vmem] * 7 + [hbm] * 5,
        out_specs=(vmem, vmem),
        scratch_shapes=[
            pltpu.VMEM((wide, columns), bf16),
            pltpu.VMEM((heads * hd, wide), bf16),
            pltpu.VMEM((slots, 2, block, hd), bf16),
            pltpu.VMEM((total_rows, wide), f32),
            pltpu.VMEM((n, 8, lane_room), f32),
            pltpu.VMEM((2, chips, rows, columns), f32),
            pltpu.VMEM((chips, rows, columns), f32),
            pltpu.VMEM((chips, rows, columns), f32),
            pltpu.VMEM((n, lanes, hd), bf16),
            pltpu.VMEM((slots, block, lanes), f32),
            pltpu.VMEM((slots, 1, lanes), f32),
            pltpu.VMEM((n, n, lanes), f32),
            pltpu.VMEM((n, 1, lanes), f32),
            pltpu.VMEM((slots, lanes, hd), f32),
            pltpu.VMEM((slots, 1, lanes), f32),
            pltpu.VMEM((2, chips, lanes, hd), f32),
            pltpu.VMEM((2, chips, 1, lanes), f32),
            pltpu.VMEM((chips, lanes, hd), f32),
            pltpu.VMEM((chips, 1, lanes), f32),
            pltpu.VMEM((chips, lanes, hd), f32),
            pltpu.VMEM((chips, 1, lanes), f32),
            pltpu.VMEM((n, lanes, hd), bf16),
            pltpu.VMEM((kvn, quarter, wide), f32),
            pltpu.VMEM((kvn, quarter, wide), f32),
            pltpu.VMEM((kvn, quarter, wide), bf16),
            dma((5,)),
            dma((n,)),
            dma((n,)),
            dma,
            dma,
            dma((chips,)),
            dma((chips,)),
            dma((n,)),
            dma((n,)),
            dma((n,)),
            dma((n,)),
            dma((2,)),
            dma((2,)),
            dma((2, chips)),
            dma((2, chips)),
            dma((n,)),
            dma((n,)),
            dma((kvn,)),
            dma((kvn,)),
            dma((kvn,)),
            dma((kvn,)),
        ],
        compiler_params=pltpu.CompilerParams(
            collective_id=0, has_side_effects=True, vmem_limit_bytes=60 * 1024 * 1024
        ),
    )(
        table,
        last,
        embeds,
        attn_gain[None, :],
        root_rows,
        cos,
        sin,
        linked,
        chosen,
        w_query,
        w_key,
        w_value,
        w_out,
        cache_kv.reshape(slots, 2, block, hd),
    )
    return out, appended.reshape(steps, here, 1, 2, hd)


def solution(mesh):
    return jax.shard_map(
        body,
        mesh=mesh,
        in_specs=(
            P(None, None, "blk"),
            P("blk"),
            P("blk", "kv"),
            P("blk", "kv"),
            P("blk", "kv"),
            P("kv", "blk"),
            P("blk", "kv", None, None, None),
            P(),
            P(),
            P(),
        ),
        out_specs=(P(None, None, "blk"), P(None, "blk", "kv", None, None)),
        check_vma=False,
    )
```

time: 256 us -> 87.5 us (0.34)
  waiting for transfers between devices: 127 us -> 0 us
  blocking collectives: 74.2 us -> 0 us
  Pallas kernels: 0 us -> 72.1 us
  matrix products: 13.6 us -> 0 us
  between operations: 14.2 us -> 0.78 us
  local copies, waits for them, and re-layouts: 13.6 us -> 6.65 us
  other arithmetic: 12 us -> 7.68 us
    pallas_call x0 -> x1, Pallas kernels: none -> 72.1 us  [body(): pl.pallas_call(functools.partial(kernel, sizes), out_shape=(jax.ShapeDtyp...]
    reduce_scatter x2 -> x0, waiting for transfers between devices: 57.7 us -> none  [the longest x1 31.2 us: body(): lax.psum_scatter(joined[:, :cut].reshape(beams * steps, heads, hd), 'blk'...]
    psum x1 -> x0, waiting for transfers between devices: 42.3 us -> none  [body(): lax.psum(partial, 'kv').reshape(beams, steps, width_part).transpose(1, 0, 2)]
    all_gather x2 -> x0, blocking collectives: 28.9 us -> none  [the longest x1 14.5 us: body(): queries = lax.all_gather(query, 'blk', axis=0, tiled=True)]
    unnamed x5 -> x0, waiting for transfers between devices: 27.3 us -> none
    pmax x1 -> x0, blocking collectives: 27.2 us -> none  [body(): lax.pmax(lax.dynamic_update_slice_in_dim(group_top, own_top, shard * rows...]
    psum x1 -> x0, blocking collectives: 18.1 us -> none  [body(): squares = lax.psum(jnp.sum(stream * stream, axis=2), 'blk')]
    dot_general x8 -> x0, matrix products: 13.6 us -> none  [the longest x1 4.08 us: body(): jnp.einsum('sqd,skd->sqk', by_group[group_of], cache_kv[:, 0, 0], preferr...]
  transfers between devices with their start and end apart: 4 -> 0, of which waited for: 4 -> 0; matrix products, arithmetic and copies ran while one was open for 3% -> 0% of each run, Pallas kernels for 0% -> 0%
where the time goes in v2:
time: 87.5 us; the launch traced here: 87.2 us
  Pallas kernels  72.1 us (82%)
  other arithmetic  7.68 us (9%)
  local copies, waits for them, and re-layouts  6.65 us (8%)
    pallas_call x1, Pallas kernels, body(): pl.pallas_call(functools.partial(kernel, sizes), out_shape=(jax.ShapeDtyp...  72.1 us
    unnamed x2, local copies, waits for them, and re-layouts  2.93 us
    reduce_sum x5, other arithmetic, pick(): return jnp.sum(jnp.where(hit, table[None, :], 0), axis=1)  2.25 us

profile of v2, /device:TPU:0, one launch (start us, length us, event | category | flops | bytes accessed | tf_op | source)
XLA Modules:
  0.0 87.2 jit_solution(12278752294152899791)
XLA Ops:
  0.8 0.8 slice_bitcast_fusion
  1.6 0.2 select_reduce_fusion.7
  1.7 0.2 select_reduce_fusion.4
  1.9 0.2 select_reduce_fusion.3
  2.3 0.1 eq.226
  2.4 0.8 select_reduce_fusion.9
  3.2 0.1 eq.236
  3.3 0.1 add.131
  3.4 0.1 stack.72
  3.5 0.1 stack.71
  3.6 0.1 stack.70
  3.7 0.1 broadcast_in_dim.174
  3.8 0.8 fusion.11
  4.7 0.1 and_convert_fusion
  4.8 0.7 reshape.340.chosen_ref
  5.5 0.7 broadcast_in_dim.176.root_ref
  6.2 1.5 %select_reduce_fusion = s32[32]{0:T(128)S(1)} fusion(s32[64,64]{1,0:T(8,128)S(1)} %add_add_fusion, s32[64,64]{1,0:T(8,128)} %param.18, s32[32]{0:T(128)S(1)} %iota_add_fusion), kind=kLoop, calls=%fused_computation | loop fusion | flops 393184 | bytes 33024 | tf_op jit(solution)/shard_map/reduce_sum | solution.py:428
  7.7 0.8 select_reduce_fusion.8
  8.6 0.2 convert_reduce_fusion
  8.8 0.1 convert_reduce_fusion.2
  8.9 0.6 pad_add_fusion.3.last_ref
  9.6 0.1 select_reduce_fusion.1
  9.7 0.1 compare_bitcast_fusion
  9.8 0.1 fusion.8
  9.9 0.6 pad_add_fusion.slot_ref
  10.5 0.1 fusion.4
  10.6 0.7 pad_maximum_fusion
  11.3 0.1 eq.234
  11.5 0.7 convert_element_type.36.linked_ref
  12.2 72.1 %shard_map.113 = (bf16[3,64,512]{2,1,0:T(8,128)(2,1)}, bf16[24,256]{1,0:T(8,128)(2,1)}) custom-call(s32[5,32]{1,0:T(8,128)} %pad_add_fusion.slot_ref, s32[2,8]{1,0:T(2,128)} %pad_add_fusion.3.last_ref, bf16[3,64,512]{2,1,0:T(8,128)(2,1)} %embeds_ref.1, f32[1,512]{1,0:T(1,128)} %bitcast.71, s32[8,1,192]{2,1,0:T(1,128)} %broadcast_in_dim.176.root_ref, ...), custom_call_target="tpu_custom_call" | custom-call | tf_op jit(solution)/shard_map/pallas_call | solution.py:488
  84.3 1.3 %copy.19 = bf16[3,8,1,2,128]{4,3,2,1,0:T(2,128)(2,1)} copy(bf16[3,8,1,2,128]{4,1,3,0,2:T(8,128)(2,1)} %bitcast.66) | data formatting | bytes 24576
  85.6 1.6 %copy.21 = bf16[3,64,512]{2,1,0:T(8,128)(2,1)} copy(bf16[3,64,512]{2,1,0:T(8,128)(2,1)} %get-tuple-element.38) | data formatting | bytes 393216
  (29 shorter events, 0.6 us)

commit v3 on v2

v3 whole, which is shorter than its diff:
```python
import functools
import math

import jax
import jax.numpy as jnp
from jax import lax
from jax.experimental import pallas as pl
from jax.experimental.pallas import tpu as pltpu
from jax.sharding import PartitionSpec as P

GROUP = 8


NEGATIVE = -1e30
EPSILON = 1e-05
ROPE_BASE = 5000000.0


MESH = pl.DeviceIdType.MESH


def remote(source, target, send, recv, axis, index):
    return pltpu.make_async_remote_copy(
        src_ref=source,
        dst_ref=target,
        send_sem=send,
        recv_sem=recv,
        device_id={axis: index},
        device_id_type=MESH,
    )


def kernel(
    sizes,
    slot_ref,
    last_ref,
    embeds_ref,
    gain_ref,
    root_ref,
    cos_ref,
    sin_ref,
    linked_ref,
    chosen_ref,
    wq_hbm,
    wk_hbm,
    wv_hbm,
    wo_hbm,
    cache_hbm,
    out_ref,
    appended_ref,
    weights,
    w_out,
    cache,
    stream,
    squares,
    part_a,
    part_b,
    sib_a,
    sib_b,
    z_a,
    z_b,
    turned,
    q_a,
    q_b,
    scores,
    seg_top,
    tops,
    ceilings,
    seg_num,
    seg_den,
    num,
    den,
    sib_num,
    sib_den,
    low_num,
    z_num,
    z_den,
    att_all,
    out_part,
    kv_part,
    out_rows,
    load_sem,
    sq_send,
    sq_recv,
    sib_send,
    sib_recv,
    z_send,
    z_recv,
    q_send,
    q_recv,
    top_send,
    top_recv,
    nsib_send,
    nsib_recv,
    nz_send,
    nz_recv,
    a_send,
    a_recv,
    kv_send,
    kv_recv,
    o_send,
    o_recv,
):
    n, kvn, steps, here, heads, hd, slots, width = sizes
    me = lax.axis_index("blk")
    kv = lax.axis_index("kv")
    chips = n // 2
    chip, core = me // 2, lax.rem(me, 2)
    sibling = me + 1 - 2 * core
    rows = steps * here
    beams = n * here
    quarter = n * rows // kvn
    half = heads // 2
    lanes = half * rows
    q_all = (q_a, q_b)
    parts, sib_parts, z_parts = (part_a, part_b), (sib_a, sib_b), (z_a, z_b)
    scaling = 1.0 / math.sqrt(hd)
    wide = w_out.shape[1]

    barrier = pltpu.get_barrier_semaphore()
    for d in range(1, n):
        pl.semaphore_signal(
            barrier, inc=1, device_id={"blk": lax.rem(me + d, n)}, device_id_type=MESH
        )
    for d in range(1, kvn):
        pl.semaphore_signal(
            barrier, inc=1, device_id={"kv": lax.rem(kv + d, kvn)}, device_id_type=MESH
        )
    hw = half * hd
    loads = [
        pltpu.make_async_copy(
            wq_hbm.at[:, pl.ds(0, hw)], weights.at[:, pl.ds(0, hw)], load_sem.at[0]
        ),
        pltpu.make_async_copy(wk_hbm, weights.at[:, pl.ds(hw, hd)], load_sem.at[1]),
        pltpu.make_async_copy(wv_hbm, weights.at[:, pl.ds(hw + hd, hd)], load_sem.at[2]),
        pltpu.make_async_copy(
            wq_hbm.at[:, pl.ds(hw, hw)], weights.at[:, pl.ds(hw + 2 * hd, hw)], load_sem.at[3]
        ),
        pltpu.make_async_copy(cache_hbm, cache, load_sem.at[4]),
        pltpu.make_async_copy(wo_hbm, w_out, load_sem.at[5]),
    ]
    for load in loads:
        load.start()

    x = embeds_ref[...].astype(jnp.float32)
    eye = lax.broadcasted_iota(jnp.int32, (beams, beams), 0) == lax.broadcasted_iota(
        jnp.int32, (beams, beams), 1
    )
    for s in range(steps):
        column = jnp.sum(x[s] * x[s], axis=1, keepdims=True)
        squares[0, s : s + 1, 0:beams] = jnp.sum(jnp.where(eye, column, 0.0), axis=0, keepdims=True)
    pl.semaphore_wait(barrier, n - 1 + kvn - 1)
    sends = []
    for d in range(1, n):
        sends.append(
            remote(
                squares.at[0], squares.at[d], sq_send.at[d], sq_recv.at[d], "blk", lax.rem(me + d, n)
            )
        )
        sends[-1].start()
    by_part = x.reshape(steps, n, here, wide).transpose(1, 0, 2, 3).reshape(n * rows, wide)
    stream[...] = by_part
    for send in sends:
        send.wait()
    normed = []
    for s in range(steps):
        total = squares[0, s : s + 1, 0:beams]
        for d in range(1, n):
            total = total + squares[d, s : s + 1, 0:beams]
        column = jnp.sum(jnp.where(eye, total, 0.0), axis=1, keepdims=True)
        normed.append(x[s] * lax.rsqrt(column / width + EPSILON) * gain_ref[...])
    normed = (
        jnp.stack(normed)
        .reshape(steps, chips, 2, here, wide)
        .transpose(2, 1, 0, 3, 4)
        .reshape(2, chips * rows, wide)
        .astype(jnp.bfloat16)
    )
    for load in loads[:4]:
        load.wait()

    def across(source, target, send_sem, recv_sem):
        copies = []
        for d in range(1, chips):
            t = lax.rem(chip + d, chips)
            copies.append(
                remote(
                    source.at[t], target.at[d], send_sem.at[d], recv_sem.at[d], "blk", 2 * t + core
                )
            )
            copies[-1].start()
        return copies

    over = []
    first_column = 0
    for k in range(2):
        span = parts[k].shape[-1]
        for c in range(2):
            parts[k][c] = jnp.dot(
                normed[c],
                weights[:, first_column : first_column + span],
                preferred_element_type=jnp.float32,
            ).reshape(sib_parts[k].shape)
        first_column += span
        over.append(
            remote(
                parts[k].at[1 - core], sib_parts[k], sib_send.at[k], sib_recv.at[k], "blk", sibling
            )
        )
        over[k].start()
    crossing = []
    for k in range(2):
        over[k].wait()
        sib_parts[k][...] = parts[k][core] + sib_parts[k][...]
        crossing.append(across(sib_parts[k], z_parts[k], z_send.at[k], z_recv.at[k]))
    loads[4].wait()

    def turn_values(i, carry):
        turned[i] = cache[i, 1].astype(jnp.float32).T.astype(jnp.bfloat16)
        return carry

    lax.fori_loop(0, slots, turn_values, 0, unroll=2)
    cos, sin = cos_ref[...], sin_ref[...]

    def rope(block):
        return block * cos + pltpu.roll(block, hd // 2, 1) * sin

    def arrived(k):
        for copy in crossing[k]:
            copy.wait()
        total = sib_parts[k][chip]
        for d in range(1, chips):
            total = total + z_parts[k][d]
        return total

    def spread(ref, send_sem, recv_sem):
        direct = []
        for d in range(1, chips):
            peer = 2 * lax.rem(chip + d, chips) + core
            direct.append(
                remote(ref.at[me], ref.at[me], send_sem.at[d], recv_sem.at[d], "blk", peer)
            )
            direct[-1].start()
        to_sibling = remote(
            ref.at[me], ref.at[me], send_sem.at[0], recv_sem.at[0], "blk", sibling
        )
        to_sibling.start()
        return direct, [to_sibling]

    def relay(ref, send_sem, recv_sem, copies):
        for d in range(1, chips):
            copies[0][d - 1].wait_recv()
            origin = 2 * lax.rem(chip + chips - d, chips) + core
            copies[1].append(
                remote(
                    ref.at[origin],
                    ref.at[origin],
                    send_sem.at[chips + d],
                    recv_sem.at[chips + d],
                    "blk",
                    sibling,
                )
            )
            copies[1][-1].start()

    def finish(copies):
        for copy in copies[1]:
            copy.wait()
        for copy in copies[0]:
            copy.wait_send()

    def turn_query(total):
        return jnp.concatenate(
            [rope(total[:, h * hd : (h + 1) * hd]) for h in range(half)], axis=0
        ).astype(jnp.bfloat16)

    queries, gathers = [None, None], [None, None]
    total = arrived(0)
    queries[0] = turn_query(total)
    q_all[0][me] = queries[0]
    gathers[0] = spread(q_all[0], q_send.at[0], q_recv.at[0])
    key = rope(total[:, half * hd : (half + 1) * hd]).astype(jnp.bfloat16)
    value_wide = total[:, (half + 1) * hd :]
    value = value_wide.astype(jnp.bfloat16)
    value_turned = value_wide.T.astype(jnp.bfloat16)
    appended_ref[...] = jnp.dot(
        chosen_ref[...],
        jnp.concatenate([key, value], axis=1),
        preferred_element_type=jnp.float32,
    ).astype(jnp.bfloat16)
    queries[1] = turn_query(arrived(1))
    q_all[1][me] = queries[1]
    gathers[1] = spread(q_all[1], q_send.at[1], q_recv.at[1])
    relay(q_all[0], q_send.at[0], q_recv.at[0], gathers[0])

    contract_last = (((1,), (1,)), ((), ()))
    block = cache.shape[2]
    token = lax.broadcasted_iota(jnp.int32, (block, lanes), 0)
    own_scores, top_sends = [], []
    for k in range(2):
        own_scores.append(
            jnp.where(
                linked_ref[...] > 0,
                lax.dot_general(
                    key, queries[k], contract_last, preferred_element_type=jnp.float32
                )
                * scaling,
                NEGATIVE,
            )
        )
        own_top = jnp.max(own_scores[k], axis=0, keepdims=True)
        finish(gathers[k])

        def look(i, top):
            group = slot_ref[1, i]
            score = (
                lax.dot_general(
                    cache[slot_ref[0, i], 0],
                    q_all[k][group],
                    contract_last,
                    preferred_element_type=jnp.float32,
                )
                * scaling
            )
            limit = jnp.where(root_ref[group] == slot_ref[2, i], slot_ref[3, i], 0)
            score = jnp.where(token < limit, score, NEGATIVE)
            scores[k, i] = score
            kept = jnp.where(slot_ref[4, i] > 0, top, NEGATIVE)
            top = jnp.maximum(kept, jnp.max(score, axis=0, keepdims=True))
            seg_top[i] = top
            return top

        lax.fori_loop(0, slots, look, jnp.full((1, lanes), NEGATIVE, jnp.float32), unroll=8)
        for g in range(n):
            top = jnp.where(last_ref[1, g] > 0, seg_top[last_ref[0, g]], NEGATIVE)
            tops[k, 0, g : g + 1, :] = jnp.where(me == g, jnp.maximum(top, own_top), top)
        copies = []
        for d in range(1, n):
            copies.append(
                remote(
                    tops.at[k, 0],
                    tops.at[k, d],
                    top_send.at[k, d],
                    top_recv.at[k, d],
                    "blk",
                    lax.rem(me + d, n),
                )
            )
            copies[-1].start()
        top_sends.append(copies)
        if k == 0:
            relay(q_all[1], q_send.at[1], q_recv.at[1], gathers[1])

    pairs, own_nums, own_dens = [], [], []

    def attend(k):
        for copy in top_sends[k]:
            copy.wait()
        ceiling = tops[k, 0]
        for d in range(1, n):
            ceiling = jnp.maximum(ceiling, tops[k, d])
        ceilings[...] = ceiling[:, None, :]

        def add(i, carry):
            total, count = carry
            probs = jnp.exp(scores[k, i] - ceilings[slot_ref[1, i]])
            same = slot_ref[4, i] > 0
            count = jnp.where(same, count, 0.0) + jnp.sum(probs, axis=0, keepdims=True)
            total = jnp.where(same, total, 0.0) + jnp.dot(
                turned[slot_ref[0, i]],
                probs.astype(jnp.bfloat16),
                preferred_element_type=jnp.float32,
            )
            seg_num[i] = total
            seg_den[i] = count
            return total, count

        lax.fori_loop(
            0,
            slots,
            add,
            (jnp.zeros((hd, lanes), jnp.float32), jnp.zeros((1, lanes), jnp.float32)),
            unroll=4,
        )
        own_probs = jnp.exp(own_scores[k] - ceilings[me])
        own_nums.append(
            jnp.dot(
                value_turned, own_probs.astype(jnp.bfloat16), preferred_element_type=jnp.float32
            ).T
        )
        own_dens.append(jnp.sum(own_probs, axis=0, keepdims=True))
        for t in range(chips):
            for c in range(2):
                g = 2 * t + c
                some = last_ref[1, g] > 0
                num[k, c, t] = jnp.where(some, seg_num[last_ref[0, g]], 0.0).T
                den[k, c, t] = jnp.where(some, seg_den[last_ref[0, g]], 0.0)
        pair = [
            remote(
                num.at[k, 1 - core],
                sib_num.at[k],
                nsib_send.at[k, 0],
                nsib_recv.at[k, 0],
                "blk",
                sibling,
            ),
            remote(
                den.at[k, 1 - core],
                sib_den.at[k],
                nsib_send.at[k, 1],
                nsib_recv.at[k, 1],
                "blk",
                sibling,
            ),
        ]
        for copy in pair:
            copy.start()
        pairs.append(pair)

    def send_sums(k):
        for copy in pairs[k]:
            copy.wait()
        sib_num[k] = sib_num[k] + num[k, core]
        sib_den[k] = sib_den[k] + den[k, core]
        low_num[k] = sib_num[k].astype(jnp.bfloat16)
        return across(low_num.at[k], z_num.at[k], nz_send.at[k, 0], nz_recv.at[k, 0]) + across(
            sib_den.at[k], z_den.at[k], nz_send.at[k, 1], nz_recv.at[k, 1]
        )

    turn = lax.broadcasted_iota(jnp.int32, (lanes, lanes), 0) == lax.broadcasted_iota(
        jnp.int32, (lanes, lanes), 1
    )

    def close(k, copies):
        for copy in copies:
            copy.wait()
        numerator = own_nums[k] + sib_num[k, chip]
        denominator = own_dens[k] + sib_den[k, chip]
        for d in range(1, chips):
            numerator = numerator + z_num[k, d].astype(jnp.float32)
            denominator = denominator + z_den[k, d]
        column = jnp.sum(jnp.where(turn, denominator, 0.0), axis=1, keepdims=True)
        att_all[k, me] = (numerator / column).astype(jnp.bfloat16)
        return spread(att_all.at[k], a_send.at[k], a_recv.at[k])

    attend(0)
    sums = [send_sums(0)]
    attend(1)
    gathers = [close(0, sums[0])]
    sums.append(send_sums(1))
    relay(att_all.at[0], a_send.at[0], a_recv.at[0], gathers[0])
    gathers.append(close(1, sums[1]))
    loads[5].wait()

    def project(k):
        finish(gathers[k])
        attended = att_all[k].astype(jnp.float32).reshape(n, half, rows, hd)
        attended = jnp.concatenate(
            [attended[:, h].reshape(n * rows, hd) for h in range(half)], axis=1
        ).astype(jnp.bfloat16)
        return jnp.dot(
            attended,
            w_out[k * half * hd : (k + 1) * half * hd, :],
            preferred_element_type=jnp.float32,
        )

    early = project(0)
    relay(att_all.at[1], a_send.at[1], a_recv.at[1], gathers[1])
    out_part[...] = (early + project(1)).reshape(out_part.shape)
    sends = []
    for d in range(1, kvn):
        t = lax.rem(kv + d, kvn)
        sends.append(
            remote(out_part.at[t], kv_part.at[d], kv_send.at[d], kv_recv.at[d], "kv", t)
        )
        sends[-1].start()
    total = out_part[kv]
    for send in sends:
        send.wait()
    for d in range(1, kvn):
        total = total + kv_part[d]
    start = pl.multiple_of(kv * quarter, 16)
    out_rows[kv] = (stream[pl.ds(start, quarter)] + total).astype(jnp.bfloat16)
    sends = []
    for d in range(1, kvn):
        t = lax.rem(kv + d, kvn)
        sends.append(
            remote(out_rows.at[kv], out_rows.at[kv], o_send.at[d], o_recv.at[d], "kv", t)
        )
        sends[-1].start()
    for send in sends:
        send.wait()
    result = out_rows[...].astype(jnp.float32).reshape(n, steps, here, wide)
    out_ref[...] = result.transpose(1, 0, 2, 3).reshape(steps, beams, wide).astype(jnp.bfloat16)


def pick(table, index):
    count = table.shape[0]
    hit = index[:, None] == jnp.arange(count, dtype=jnp.int32)[None, :]
    return jnp.sum(jnp.where(hit, table[None, :], 0), axis=1)


def body(
    embeds, attn_gain, w_query, w_key, w_value, w_out, cache_kv, lengths, block_table, parents
):
    n = lax.axis_size("blk")
    kvn = lax.axis_size("kv")
    shard = lax.axis_index("blk")
    steps, beams, wide = embeds.shape
    here = beams // n
    slots = cache_kv.shape[0]
    block, hd = cache_kv.shape[3], cache_kv.shape[4]
    heads = w_query.shape[1] // hd
    rows = here * steps
    half = heads // 2
    lanes = half * rows
    all_beams = jnp.arange(beams, dtype=jnp.int32)
    roots, origin = [], []
    for s in range(steps):
        before = roots[-1] if s else all_beams
        roots.append(pick(before, parents[s]))
        origin.append([pick(line, parents[s]) for line in (origin[-1] if s else [])] + [all_beams])
    root = jnp.stack(roots)
    slot_ids = shard * slots + jnp.arange(slots, dtype=jnp.int32)
    named = block_table[None] == slot_ids[:, None, None]
    code = jnp.arange(block_table.size, dtype=jnp.int32).reshape(block_table.shape) + 1
    code = jnp.sum(jnp.where(named, code[None], 0), axis=(1, 2)) - 1
    filled = code >= 0
    owner = jnp.where(filled, code // block_table.shape[1], -1)
    logical = code % block_table.shape[1]
    tokens = jnp.where(filled, pick(lengths, jnp.maximum(owner, 0)) - logical * block, 0)
    group = jnp.where(filled, owner // GROUP, n - 1)
    place = jnp.arange(slots, dtype=jnp.int32)
    rank = jnp.sum(
        (group[None, :] < group[:, None])
        | ((group[None, :] == group[:, None]) & (place[None, :] < place[:, None])),
        axis=1,
    )
    table = jnp.stack([place, group, owner, tokens])
    table = jnp.sum(jnp.where((rank[:, None] == place[None, :])[None], table[:, :, None], 0), axis=1)
    same = jnp.concatenate(
        [jnp.zeros((1,), jnp.int32), (table[1, 1:] == table[1, :-1]).astype(jnp.int32)]
    )
    table = jnp.concatenate([table, same[None]])
    upto = jnp.sum(group[None, :] <= jnp.arange(n, dtype=jnp.int32)[:, None], axis=1)
    held = jnp.sum(group[None, :] == jnp.arange(n, dtype=jnp.int32)[:, None], axis=1)
    last = jnp.stack([jnp.maximum(upto - 1, 0), held]).astype(jnp.int32)

    root_rows = root.reshape(steps, n, here).transpose(1, 0, 2).reshape(n, 1, 1, rows)
    root_rows = jnp.broadcast_to(root_rows, (n, 1, half, rows)).reshape(n, 1, lanes)
    own = lax.dynamic_slice_in_dim(root, shard * here, here, 1)
    position = pick(lengths, own.reshape(-1)).reshape(steps, here) + jnp.arange(
        steps, dtype=jnp.int32
    )[:, None]
    exponent = jnp.arange(hd // 2, dtype=jnp.float32) * (2.0 / hd)
    angles = position.reshape(rows).astype(jnp.float32)[:, None] * (ROPE_BASE ** (-exponent))
    cos, sin = jnp.cos(angles), jnp.sin(angles)
    cos = jnp.concatenate([cos, cos], axis=1)
    sin = jnp.concatenate([-sin, sin], axis=1)
    origin_own = jnp.stack(
        [
            jnp.stack([origin[s][u] if u <= s else all_beams * 0 - 1 for u in range(steps)])
            for s in range(steps)
        ]
    )
    origin_own = lax.dynamic_slice_in_dim(origin_own, shard * here, here, 2) - shard * here
    seat = jnp.arange(here, dtype=jnp.int32)
    meets = origin_own.transpose(0, 2, 1)[:, :, :, None] == seat
    linked = meets.transpose(2, 3, 0, 1).reshape(rows, 1, rows)
    linked = jnp.broadcast_to(linked, (rows, half, rows)).reshape(rows, lanes).astype(jnp.float32)
    chosen = meets[-1].transpose(1, 0, 2)[:, :, None, :] & (
        jnp.arange(steps)[:, None, None, None] == jnp.arange(steps)[None, None, :, None]
    )
    chosen = chosen.reshape(rows, rows).astype(jnp.bfloat16)

    chips = n // 2
    total_rows = n * rows
    columns = (heads + 2) * hd
    quarter = total_rows // kvn
    sizes = (n, kvn, steps, here, heads, hd, slots, wide * n)
    bf16, f32 = jnp.bfloat16, jnp.float32
    dma = pltpu.SemaphoreType.DMA
    lane_room = -(-beams // 128) * 128
    vmem = pl.BlockSpec(memory_space=pltpu.VMEM)
    smem = pl.BlockSpec(memory_space=pltpu.SMEM)
    hbm = pl.BlockSpec(memory_space=pl.ANY)
    out, appended = pl.pallas_call(
        functools.partial(kernel, sizes),
        out_shape=(
            jax.ShapeDtypeStruct((steps, beams, wide), bf16),
            jax.ShapeDtypeStruct((rows, 2 * hd), bf16),
        ),
        in_specs=[smem, smem] + [vmem] * 7 + [hbm] * 5,
        out_specs=(vmem, vmem),
        scratch_shapes=[
            pltpu.VMEM((wide, columns), bf16),
            pltpu.VMEM((heads * hd, wide), bf16),
            pltpu.VMEM((slots, 2, block, hd), bf16),
            pltpu.VMEM((total_rows, wide), f32),
            pltpu.VMEM((n, 8, lane_room), f32),
            pltpu.VMEM((2, chips, rows, (half + 2) * hd), f32),
            pltpu.VMEM((2, chips, rows, half * hd), f32),
            pltpu.VMEM((chips, rows, (half + 2) * hd), f32),
            pltpu.VMEM((chips, rows, half * hd), f32),
            pltpu.VMEM((chips, rows, (half + 2) * hd), f32),
            pltpu.VMEM((chips, rows, half * hd), f32),
            pltpu.VMEM((slots, hd, block), bf16),
            pltpu.VMEM((n, lanes, hd), bf16),
            pltpu.VMEM((n, lanes, hd), bf16),
            pltpu.VMEM((2, slots, block, lanes), f32),
            pltpu.VMEM((slots, 1, lanes), f32),
            pltpu.VMEM((2, n, n, lanes), f32),
            pltpu.VMEM((n, 1, lanes), f32),
            pltpu.VMEM((slots, hd, lanes), f32),
            pltpu.VMEM((slots, 1, lanes), f32),
            pltpu.VMEM((2, 2, chips, lanes, hd), f32),
            pltpu.VMEM((2, 2, chips, 1, lanes), f32),
            pltpu.VMEM((2, chips, lanes, hd), f32),
            pltpu.VMEM((2, chips, 1, lanes), f32),
            pltpu.VMEM((2, chips, lanes, hd), bf16),
            pltpu.VMEM((2, chips, lanes, hd), bf16),
            pltpu.VMEM((2, chips, 1, lanes), f32),
            pltpu.VMEM((2, n, lanes, hd), bf16),
            pltpu.VMEM((kvn, quarter, wide), f32),
            pltpu.VMEM((kvn, quarter, wide), f32),
            pltpu.VMEM((kvn, quarter, wide), bf16),
            dma((6,)),
            dma((n,)),
            dma((n,)),
            dma((2,)),
            dma((2,)),
            dma((2, chips)),
            dma((2, chips)),
            dma((2, n)),
            dma((2, n)),
            dma((2, n)),
            dma((2, n)),
            dma((2, 2)),
            dma((2, 2)),
            dma((2, 2, chips)),
            dma((2, 2, chips)),
            dma((2, n)),
            dma((2, n)),
            dma((kvn,)),
            dma((kvn,)),
            dma((kvn,)),
            dma((kvn,)),
        ],
        compiler_params=pltpu.CompilerParams(
            collective_id=0, has_side_effects=True, vmem_limit_bytes=60 * 1024 * 1024
        ),
    )(
        table,
        last,
        embeds,
        attn_gain[None, :],
        root_rows,
        cos,
        sin,
        linked,
        chosen,
        w_query,
        w_key,
        w_value,
        w_out,
        cache_kv.reshape(slots, 2, block, hd),
    )
    return out, appended.reshape(steps, here, 1, 2, hd)


def solution(mesh):
    return jax.shard_map(
        body,
        mesh=mesh,
        in_specs=(
            P(None, None, "blk"),
            P("blk"),
            P("blk", "kv"),
            P("blk", "kv"),
            P("blk", "kv"),
            P("kv", "blk"),
            P("blk", "kv", None, None, None),
            P(),
            P(),
            P(),
        ),
        out_specs=(P(None, None, "blk"), P(None, "blk", "kv", None, None)),
        check_vma=False,
    )
```

time: 87.5 us -> 80.2 us (0.917)
  Pallas kernels: 72.1 us -> 64.8 us
    pallas_call x1, Pallas kernels: 72.1 us -> 64.8 us  [body(): pl.pallas_call(functools.partial(kernel, sizes), out_shape=(jax.ShapeDtyp...]
where the time goes in v3:
time: 80.2 us; the launch traced here: 79.9 us
  Pallas kernels  64.8 us (81%)
  other arithmetic  7.68 us (10%)
  local copies, waits for them, and re-layouts  6.63 us (8%)
    pallas_call x1, Pallas kernels, body(): pl.pallas_call(functools.partial(kernel, sizes), out_shape=(jax.ShapeDtyp...  64.8 us
    unnamed x2, local copies, waits for them, and re-layouts  2.93 us
    reduce_sum x5, other arithmetic, pick(): return jnp.sum(jnp.where(hit, table[None, :], 0), axis=1)  2.25 us

profile of v3, /device:TPU:0, one launch (start us, length us, event | category | flops | bytes accessed | tf_op | source)
XLA Modules:
  0.0 79.9 jit_solution(11616682719091552598)
XLA Ops:
  0.8 0.8 slice_bitcast_fusion
  1.6 0.2 select_reduce_fusion.7
  1.7 0.2 select_reduce_fusion.4
  1.9 0.2 select_reduce_fusion.3
  2.3 0.1 eq.226
  2.4 0.8 %select_reduce_fusion.9 = s32[24]{0:T(128)S(1)} fusion(s32[64]{0:T(128)} %param.17, s32[24]{0:T(128)S(1)} %eq.226), kind=kLoop, calls=%fused_computation.26 | loop fusion | flops 4584 | bytes 448 | tf_op jit(solution)/shard_map/reduce_sum | solution.py:500
  3.2 0.1 eq.236
  3.3 0.1 add.131
  3.4 0.1 stack.72
  3.5 0.1 stack.71
  3.6 0.1 stack.70
  3.7 0.1 broadcast_in_dim.174
  3.8 0.8 %fusion.11 = (s32[3,8,3]{1,2,0:T(4,128)S(1)}, s32[3,3,8]{2,0,1:T(4,128)S(1)}) fusion(s32[]{:T(128)S(6)} %mul.47, s32[]{:T(128)S(6)} %select_n.164, s32[1,3,64]{2,1,0:T(4,128)S(1)} %get-tuple-element.35, s32[1,3,64]{2,1,0:T(4,128)S(1)} %get-tuple-element.34, s32[1,3,64]{2,1,0:T(4,128)} %constant.70.clone.1), kind=kLoop, calls=%fused_computation.84 | loop fusion | flops 432 | bytes 2888 | tf_op jit(solution)/shard_map/transpose | solution.py:568
  4.7 0.7 broadcast_in_dim.176.root_ref
  5.4 0.1 and_convert_fusion
  5.5 0.7 reshape.340.chosen_ref
  6.2 1.5 %select_reduce_fusion = s32[32]{0:T(128)S(1)} fusion(s32[64,64]{1,0:T(8,128)S(1)} %add_add_fusion, s32[64,64]{1,0:T(8,128)} %param.18, s32[32]{0:T(128)S(1)} %iota_add_fusion), kind=kLoop, calls=%fused_computation | loop fusion | flops 393184 | bytes 33024 | tf_op jit(solution)/shard_map/reduce_sum | solution.py:527
  7.7 0.8 %select_reduce_fusion.8 = s32[32]{0:T(128)S(1)} fusion(s32[64]{0:T(128)} %param.17, s32[32]{0:T(128)S(1)} %broadcast_maximum_fusion), kind=kLoop, calls=%fused_computation.15 | loop fusion | flops 6112 | bytes 512 | tf_op jit(solution)/shard_map/reduce_sum | solution.py:500
  8.6 0.2 convert_reduce_fusion
  8.8 0.1 convert_reduce_fusion.2
  8.9 0.6 pad_add_fusion.3.last_ref
  9.6 0.1 select_reduce_fusion.1
  9.7 0.1 compare_bitcast_fusion
  9.8 0.1 fusion.8
  9.9 0.6 pad_add_fusion.slot_ref
  10.5 0.1 fusion.4
  10.6 0.7 pad_maximum_fusion
  11.3 0.1 eq.234
  11.5 0.7 convert_element_type.36.linked_ref
  12.2 64.8 %shard_map.113 = (bf16[3,64,512]{2,1,0:T(8,128)(2,1)}, bf16[24,256]{1,0:T(8,128)(2,1)}) custom-call(s32[5,32]{1,0:T(8,128)} %pad_add_fusion.slot_ref, s32[2,8]{1,0:T(2,128)} %pad_add_fusion.3.last_ref, bf16[3,64,512]{2,1,0:T(8,128)(2,1)} %embeds_ref.1, f32[1,512]{1,0:T(1,128)} %bitcast.71, s32[8,1,96]{2,1,0:T(1,128)} %broadcast_in_dim.176.root_ref, ...), custom_call_target="tpu_custom_call" | custom-call | tf_op jit(solution)/shard_map/pallas_call | solution.py:587
  76.9 1.3 %copy.19 = bf16[3,8,1,2,128]{4,3,2,1,0:T(2,128)(2,1)} copy(bf16[3,8,1,2,128]{4,1,3,0,2:T(8,128)(2,1)} %bitcast.66) | data formatting | bytes 24576
  78.3 1.6 %copy.21 = bf16[3,64,512]{2,1,0:T(8,128)(2,1)} copy(bf16[3,64,512]{2,1,0:T(8,128)(2,1)} %get-tuple-element.38) | data formatting | bytes 393216
  (29 shorter events, 0.6 us)

commit v4 on v3

--- a/solution.py
+++ b/solution.py
@@ -33,14 +33,11 @@
 def kernel(
     sizes,
     slot_ref,
-    last_ref,
     embeds_ref,
     gain_ref,
-    root_ref,
+    info_ref,
     cos_ref,
     sin_ref,
-    linked_ref,
-    chosen_ref,
     wq_hbm,
     wk_hbm,
     wv_hbm,
@@ -77,6 +74,7 @@
     z_den,
     att_all,
     out_part,
+    own_part,
     kv_part,
     out_rows,
     load_sem,
@@ -173,7 +171,7 @@
         jnp.stack(normed)
         .reshape(steps, chips, 2, here, wide)
         .transpose(2, 1, 0, 3, 4)
-        .reshape(2, chips * rows, wide)
+        .reshape(n * rows, wide)
         .astype(jnp.bfloat16)
     )
     for load in loads[:4]:
@@ -195,12 +193,9 @@
     first_column = 0
     for k in range(2):
         span = parts[k].shape[-1]
-        for c in range(2):
-            parts[k][c] = jnp.dot(
-                normed[c],
-                weights[:, first_column : first_column + span],
-                preferred_element_type=jnp.float32,
-            ).reshape(sib_parts[k].shape)
+        parts[k][...] = jnp.dot(
+            normed, weights[:, first_column : first_column + span], preferred_element_type=jnp.float32
+        ).reshape(parts[k].shape)
         first_column += span
         over.append(
             remote(
@@ -283,10 +278,18 @@
     value_wide = total[:, (half + 1) * hd :]
     value = value_wide.astype(jnp.bfloat16)
     value_turned = value_wide.T.astype(jnp.bfloat16)
+    entry = lax.broadcasted_iota(jnp.int32, (rows, lanes), 0)
+    linked = jnp.zeros((rows, lanes), jnp.float32)
+    for u in range(steps):
+        seat = info_ref[me, 1 + u : 2 + u, :] + u * here
+        known = info_ref[me, 1 + u : 2 + u, :] >= 0
+        linked = jnp.where((entry == seat) & known, 1.0, linked)
+    final = jnp.concatenate([linked[:, rows - here : rows]] * steps, axis=1)
+    source = lax.broadcasted_iota(jnp.int32, (rows, rows), 0) // here
+    wanted = lax.broadcasted_iota(jnp.int32, (rows, rows), 1) // here
+    chosen = jnp.where(source == wanted, final, 0.0).T.astype(jnp.bfloat16)
     appended_ref[...] = jnp.dot(
-        chosen_ref[...],
-        jnp.concatenate([key, value], axis=1),
-        preferred_element_type=jnp.float32,
+        chosen, jnp.concatenate([key, value], axis=1), preferred_element_type=jnp.float32
     ).astype(jnp.bfloat16)
     queries[1] = turn_query(arrived(1))
     q_all[1][me] = queries[1]
@@ -300,7 +303,7 @@
     for k in range(2):
         own_scores.append(
             jnp.where(
-                linked_ref[...] > 0,
+                linked > 0,
                 lax.dot_general(
                     key, queries[k], contract_last, preferred_element_type=jnp.float32
                 )
@@ -312,27 +315,27 @@
         finish(gathers[k])
 
         def look(i, top):
-            group = slot_ref[1, i]
+            group = slot_ref[1 * slots + i]
             score = (
                 lax.dot_general(
-                    cache[slot_ref[0, i], 0],
+                    cache[slot_ref[i], 0],
                     q_all[k][group],
                     contract_last,
                     preferred_element_type=jnp.float32,
                 )
                 * scaling
             )
-            limit = jnp.where(root_ref[group] == slot_ref[2, i], slot_ref[3, i], 0)
+            limit = jnp.where(info_ref[group, 0:1, :] == slot_ref[2 * slots + i], slot_ref[3 * slots + i], 0)
             score = jnp.where(token < limit, score, NEGATIVE)
             scores[k, i] = score
-            kept = jnp.where(slot_ref[4, i] > 0, top, NEGATIVE)
+            kept = jnp.where(slot_ref[4 * slots + i] > 0, top, NEGATIVE)
             top = jnp.maximum(kept, jnp.max(score, axis=0, keepdims=True))
             seg_top[i] = top
             return top
 
-        lax.fori_loop(0, slots, look, jnp.full((1, lanes), NEGATIVE, jnp.float32), unroll=8)
+        lax.fori_loop(0, slots, look, jnp.full((1, lanes), NEGATIVE, jnp.float32), unroll=16)
         for g in range(n):
-            top = jnp.where(last_ref[1, g] > 0, seg_top[last_ref[0, g]], NEGATIVE)
+            top = jnp.where(slot_ref[5 * slots + n + g] > 0, seg_top[slot_ref[5 * slots + g]], NEGATIVE)
             tops[k, 0, g : g + 1, :] = jnp.where(me == g, jnp.maximum(top, own_top), top)
         copies = []
         for d in range(1, n):
@@ -363,11 +366,11 @@
 
         def add(i, carry):
             total, count = carry
-            probs = jnp.exp(scores[k, i] - ceilings[slot_ref[1, i]])
-            same = slot_ref[4, i] > 0
+            probs = jnp.exp(scores[k, i] - ceilings[slot_ref[1 * slots + i]])
+            same = slot_ref[4 * slots + i] > 0
             count = jnp.where(same, count, 0.0) + jnp.sum(probs, axis=0, keepdims=True)
             total = jnp.where(same, total, 0.0) + jnp.dot(
-                turned[slot_ref[0, i]],
+                turned[slot_ref[i]],
                 probs.astype(jnp.bfloat16),
                 preferred_element_type=jnp.float32,
             )
@@ -380,7 +383,7 @@
             slots,
             add,
             (jnp.zeros((hd, lanes), jnp.float32), jnp.zeros((1, lanes), jnp.float32)),
-            unroll=4,
+            unroll=8,
         )
         own_probs = jnp.exp(own_scores[k] - ceilings[me])
         own_nums.append(
@@ -392,9 +395,9 @@
         for t in range(chips):
             for c in range(2):
                 g = 2 * t + c
-                some = last_ref[1, g] > 0
-                num[k, c, t] = jnp.where(some, seg_num[last_ref[0, g]], 0.0).T
-                den[k, c, t] = jnp.where(some, seg_den[last_ref[0, g]], 0.0)
+                some = slot_ref[5 * slots + n + g] > 0
+                num[k, c, t] = jnp.where(some, seg_num[slot_ref[5 * slots + g]], 0.0).T
+                den[k, c, t] = jnp.where(some, seg_den[slot_ref[5 * slots + g]], 0.0)
         pair = [
             remote(
                 num.at[k, 1 - core],
@@ -466,7 +469,9 @@
 
     early = project(0)
     relay(att_all.at[1], a_send.at[1], a_recv.at[1], gathers[1])
-    out_part[...] = (early + project(1)).reshape(out_part.shape)
+    out_sum = (early + project(1)).reshape(out_part.shape)
+    out_part[...] = out_sum.astype(jnp.bfloat16)
+    own_part[...] = out_sum
     sends = []
     for d in range(1, kvn):
         t = lax.rem(kv + d, kvn)
@@ -474,11 +479,11 @@
             remote(out_part.at[t], kv_part.at[d], kv_send.at[d], kv_recv.at[d], "kv", t)
         )
         sends[-1].start()
-    total = out_part[kv]
+    total = own_part[kv]
     for send in sends:
         send.wait()
     for d in range(1, kvn):
-        total = total + kv_part[d]
+        total = total + kv_part[d].astype(jnp.float32)
     start = pl.multiple_of(kv * quarter, 16)
     out_rows[kv] = (stream[pl.ds(start, quarter)] + total).astype(jnp.bfloat16)
     sends = []
@@ -531,47 +536,36 @@
     tokens = jnp.where(filled, pick(lengths, jnp.maximum(owner, 0)) - logical * block, 0)
     group = jnp.where(filled, owner // GROUP, n - 1)
     place = jnp.arange(slots, dtype=jnp.int32)
-    rank = jnp.sum(
-        (group[None, :] < group[:, None])
-        | ((group[None, :] == group[:, None]) & (place[None, :] < place[:, None])),
-        axis=1,
-    )
-    table = jnp.stack([place, group, owner, tokens])
+    before = (group[None, :] == group[:, None]) & (place[None, :] < place[:, None])
+    rank = jnp.sum((group[None, :] < group[:, None]) | before, axis=1)
+    same = jnp.sum(before, axis=1)
+    table = jnp.stack([place, group, owner, tokens, same.astype(jnp.int32)])
     table = jnp.sum(jnp.where((rank[:, None] == place[None, :])[None], table[:, :, None], 0), axis=1)
-    same = jnp.concatenate(
-        [jnp.zeros((1,), jnp.int32), (table[1, 1:] == table[1, :-1]).astype(jnp.int32)]
-    )
-    table = jnp.concatenate([table, same[None]])
-    upto = jnp.sum(group[None, :] <= jnp.arange(n, dtype=jnp.int32)[:, None], axis=1)
-    held = jnp.sum(group[None, :] == jnp.arange(n, dtype=jnp.int32)[:, None], axis=1)
-    last = jnp.stack([jnp.maximum(upto - 1, 0), held]).astype(jnp.int32)
-
-    root_rows = root.reshape(steps, n, here).transpose(1, 0, 2).reshape(n, 1, 1, rows)
-    root_rows = jnp.broadcast_to(root_rows, (n, 1, half, rows)).reshape(n, 1, lanes)
+    every = jnp.arange(n, dtype=jnp.int32)[:, None]
+    upto = jnp.sum(group[None, :] <= every, axis=1)
+    held = jnp.sum(group[None, :] == every, axis=1)
+    table = jnp.concatenate(
+        [table.reshape(-1), jnp.maximum(upto - 1, 0), held], dtype=jnp.int32
+    )
+    base = all_beams // here * here
+    info = jnp.stack(
+        [
+            jnp.stack([roots[s] if u < 0 else origin[s][u] - base if u <= s else base * 0 - 1
+                       for s in range(steps)])
+            for u in range(-1, steps)
+        ]
+    )
+    info = info.reshape(1 + steps, steps, n, here).transpose(2, 0, 1, 3).reshape(n, 1 + steps, 1, rows)
+    info = jnp.broadcast_to(info, (n, 1 + steps, half, rows)).reshape(n, 1 + steps, lanes)
     own = lax.dynamic_slice_in_dim(root, shard * here, here, 1)
     position = pick(lengths, own.reshape(-1)).reshape(steps, here) + jnp.arange(
         steps, dtype=jnp.int32
     )[:, None]
-    exponent = jnp.arange(hd // 2, dtype=jnp.float32) * (2.0 / hd)
+    lane = jnp.arange(hd, dtype=jnp.int32)
+    exponent = (lane % (hd // 2)).astype(jnp.float32) * (2.0 / hd)
     angles = position.reshape(rows).astype(jnp.float32)[:, None] * (ROPE_BASE ** (-exponent))
-    cos, sin = jnp.cos(angles), jnp.sin(angles)
-    cos = jnp.concatenate([cos, cos], axis=1)
-    sin = jnp.concatenate([-sin, sin], axis=1)
-    origin_own = jnp.stack(
-        [
-            jnp.stack([origin[s][u] if u <= s else all_beams * 0 - 1 for u in range(steps)])
-            for s in range(steps)
-        ]
-    )
-    origin_own = lax.dynamic_slice_in_dim(origin_own, shard * here, here, 2) - shard * here
-    seat = jnp.arange(here, dtype=jnp.int32)
-    meets = origin_own.transpose(0, 2, 1)[:, :, :, None] == seat
-    linked = meets.transpose(2, 3, 0, 1).reshape(rows, 1, rows)
-    linked = jnp.broadcast_to(linked, (rows, half, rows)).reshape(rows, lanes).astype(jnp.float32)
-    chosen = meets[-1].transpose(1, 0, 2)[:, :, None, :] & (
-        jnp.arange(steps)[:, None, None, None] == jnp.arange(steps)[None, None, :, None]
-    )
-    chosen = chosen.reshape(rows, rows).astype(jnp.bfloat16)
+    cos = jnp.cos(angles)
+    sin = jnp.sin(angles) * jnp.where(lane < hd // 2, -1.0, 1.0)
 
     chips = n // 2
     total_rows = n * rows
@@ -590,7 +584,7 @@
             jax.ShapeDtypeStruct((steps, beams, wide), bf16),
             jax.ShapeDtypeStruct((rows, 2 * hd), bf16),
         ),
-        in_specs=[smem, smem] + [vmem] * 7 + [hbm] * 5,
+        in_specs=[smem] + [vmem] * 5 + [hbm] * 5,
         out_specs=(vmem, vmem),
         scratch_shapes=[
             pltpu.VMEM((wide, columns), bf16),
@@ -621,8 +615,9 @@
             pltpu.VMEM((2, chips, lanes, hd), bf16),
             pltpu.VMEM((2, chips, 1, lanes), f32),
             pltpu.VMEM((2, n, lanes, hd), bf16),
+            pltpu.VMEM((kvn, quarter, wide), bf16),
             pltpu.VMEM((kvn, quarter, wide), f32),
-            pltpu.VMEM((kvn, quarter, wide), f32),
+            pltpu.VMEM((kvn, quarter, wide), bf16),
             pltpu.VMEM((kvn, quarter, wide), bf16),
             dma((6,)),
             dma((n,)),
@@ -651,14 +646,11 @@
         ),
     )(
         table,
-        last,
         embeds,
         attn_gain[None, :],
-        root_rows,
+        info,
         cos,
         sin,
-        linked,
-        chosen,
         w_query,
         w_key,
         w_value,

time: 80.2 us -> 74.3 us (0.926)
  Pallas kernels: 64.8 us -> 62 us
  other arithmetic: 7.68 us -> 5.76 us
  local copies, waits for them, and re-layouts: 6.63 us -> 5.47 us
    pallas_call x1, Pallas kernels: 64.8 us -> 62 us  [body(): pl.pallas_call(functools.partial(kernel, sizes), out_shape=(jax.ShapeDtyp...]
    convert_element_type x2 -> x0, local copies, waits for them, and re-layouts: 1.37 us -> none  [the longest x1 0.69 us: body(): jnp.broadcast_to(linked, (rows, half, rows)).reshape(rows, lanes)]
    transpose x3 -> x1, other arithmetic: 0.92 us -> 0.01 us  [body(): info.reshape(1 + steps, steps, n, here).transpose(2, 0, 1, 3)]
where the time goes in v4:
time: 74.3 us; the launch traced here: 74 us
  Pallas kernels  62 us (83%)
  other arithmetic  5.76 us (8%)
  local copies, waits for them, and re-layouts  5.47 us (7%)
  between operations  0.77 us (1%)
    pallas_call x1, Pallas kernels, body(): pl.pallas_call(functools.partial(kernel, sizes), out_shape=(jax.ShapeDtyp...  62 us
    unnamed x2, local copies, waits for them, and re-layouts  2.93 us
    reduce_sum x5, other arithmetic, pick(): return jnp.sum(jnp.where(hit, table[None, :], 0), axis=1)  2.25 us
    reduce_sum x1, other arithmetic, body(): code = jnp.sum(jnp.where(named, code[None], 0), axis=(1, 2)) - 1  1.51 us

profile of v4, /device:TPU:0, one launch (start us, length us, event | category | flops | bytes accessed | tf_op | source)
XLA Modules:
  0.0 74.0 jit_solution(4368392620794392840)
XLA Ops:
  0.7 0.8 %slice_bitcast_fusion = (s32[64]{0:T(128)S(1)}, s32[64]{0:T(128)S(1)}, s32[64]{0:T(128)S(1)}) fusion(s32[3,64]{1,0:T(4,128)} %param.19), kind=kLoop, calls=%fused_computation.78 | loop fusion | bytes 1536 | tf_op jit(solution)/shard_map/eq | solution.py:504
  1.5 0.2 select_reduce_fusion.7
  1.7 0.2 select_reduce_fusion.6
  1.9 0.2 select_reduce_fusion.5
  2.1 0.1 constant_dynamic-slice_fusion
  2.2 0.1 eq.175
  2.3 0.8 %select_reduce_fusion.9 = s32[24]{0:T(128)S(1)} fusion(s32[64]{0:T(128)} %param.17, s32[24]{0:T(128)S(1)} %eq.175), kind=kLoop, calls=%fused_computation.23 | loop fusion | flops 4584 | bytes 448 | tf_op jit(solution)/shard_map/reduce_sum | solution.py:505
  3.1 0.1 add.190
  3.2 0.1 reduce_sum.150
  3.3 0.1 reduce_sum.146
  3.3 0.1 reduce_sum.148
  3.5 0.1 stack.64
  3.5 0.1 stack.63
  3.6 0.1 stack.62
  3.7 0.1 stack.69
  3.8 0.1 reshape.431
  3.9 0.7 fusion.1
  4.7 1.5 %select_reduce_fusion = s32[32]{0:T(128)S(1)} fusion(s32[64,64]{1,0:T(8,128)S(1)} %add_add_fusion, s32[64,64]{1,0:T(8,128)} %param.18, s32[32]{0:T(128)S(1)} %iota_add_fusion), kind=kLoop, calls=%fused_computation | loop fusion | flops 393184 | bytes 33024 | tf_op jit(solution)/shard_map/reduce_sum | solution.py:532
  6.2 0.8 %select_reduce_fusion.8 = s32[32]{0:T(128)S(1)} fusion(s32[64]{0:T(128)} %param.17, s32[32]{0:T(128)S(1)} %get-tuple-element.21), kind=kLoop, calls=%fused_computation.16 | loop fusion | flops 6112 | bytes 512 | tf_op jit(solution)/shard_map/reduce_sum | solution.py:505
  7.1 0.1 convert_reduce_fusion.3
  7.2 0.2 convert_reduce_fusion.1
  7.5 0.1 iota_compare_fusion.4
  7.5 0.1 select_reduce_fusion.1
  7.6 0.1 reshape.427
  7.7 0.6 pad_add_fusion.1.slot_ref
  8.3 0.7 reshape.428.info_ref
  9.1 62.0 %shard_map.113 = (bf16[3,64,512]{2,1,0:T(8,128)(2,1)}, bf16[24,256]{1,0:T(8,128)(2,1)}) custom-call(s32[176]{0:T(256)} %pad_add_fusion.1.slot_ref, bf16[3,64,512]{2,1,0:T(8,128)(2,1)} %embeds_ref.1, f32[1,512]{1,0:T(1,128)} %bitcast.48, s32[8,4,96]{2,1,0:T(4,128)} %reshape.428.info_ref, f32[24,128]{1,0:T(8,128)} %get-tuple-element.27.cos_ref, ...), custom_call_target="tpu_custom_call" | custom-call | tf_op jit(solution)/shard_map/pallas_call | solution.py:581
  71.0 1.3 %copy.18 = bf16[3,8,1,2,128]{4,3,2,1,0:T(2,128)(2,1)} copy(bf16[3,8,1,2,128]{4,1,3,0,2:T(8,128)(2,1)} %bitcast.44) | data formatting | bytes 24576
  72.4 1.6 %copy.22 = bf16[3,64,512]{2,1,0:T(8,128)(2,1)} copy(bf16[3,64,512]{2,1,0:T(8,128)(2,1)} %get-tuple-element.39) | data formatting | bytes 393216
  (20 shorter events, 0.2 us)

commit v5 on v4

--- a/solution.py
+++ b/solution.py
@@ -333,7 +333,12 @@
             seg_top[i] = top
             return top
 
-        lax.fori_loop(0, slots, look, jnp.full((1, lanes), NEGATIVE, jnp.float32), unroll=16)
+        top = lax.fori_loop(
+            0, slots // 2, look, jnp.full((1, lanes), NEGATIVE, jnp.float32), unroll=16
+        )
+        if k == 0:
+            relay(q_all[1], q_send.at[1], q_recv.at[1], gathers[1])
+        lax.fori_loop(slots // 2, slots, look, top, unroll=16)
         for g in range(n):
             top = jnp.where(slot_ref[5 * slots + n + g] > 0, seg_top[slot_ref[5 * slots + g]], NEGATIVE)
             tops[k, 0, g : g + 1, :] = jnp.where(me == g, jnp.maximum(top, own_top), top)
@@ -351,12 +356,10 @@
             )
             copies[-1].start()
         top_sends.append(copies)
-        if k == 0:
-            relay(q_all[1], q_send.at[1], q_recv.at[1], gathers[1])
 
     pairs, own_nums, own_dens = [], [], []
 
-    def attend(k):
+    def attend(k, between):
         for copy in top_sends[k]:
             copy.wait()
         ceiling = tops[k, 0]
@@ -378,13 +381,15 @@
             seg_den[i] = count
             return total, count
 
-        lax.fori_loop(
+        carry = lax.fori_loop(
             0,
-            slots,
+            slots // 2,
             add,
             (jnp.zeros((hd, lanes), jnp.float32), jnp.zeros((1, lanes), jnp.float32)),
             unroll=8,
         )
+        between()
+        lax.fori_loop(slots // 2, slots, add, carry, unroll=8)
         own_probs = jnp.exp(own_scores[k] - ceilings[me])
         own_nums.append(
             jnp.dot(
@@ -446,57 +451,81 @@
         att_all[k, me] = (numerator / column).astype(jnp.bfloat16)
         return spread(att_all.at[k], a_send.at[k], a_recv.at[k])
 
-    attend(0)
-    sums = [send_sums(0)]
-    attend(1)
+    sums = []
+    attend(0, lambda: None)
+    attend(1, lambda: sums.append(send_sums(0)))
     gathers = [close(0, sums[0])]
     sums.append(send_sums(1))
     relay(att_all.at[0], a_send.at[0], a_recv.at[0], gathers[0])
     gathers.append(close(1, sums[1]))
     loads[5].wait()
 
-    def project(k):
+    def gathered(k):
         finish(gathers[k])
         attended = att_all[k].astype(jnp.float32).reshape(n, half, rows, hd)
-        attended = jnp.concatenate(
+        return jnp.concatenate(
             [attended[:, h].reshape(n * rows, hd) for h in range(half)], axis=1
         ).astype(jnp.bfloat16)
-        return jnp.dot(
-            attended,
-            w_out[k * half * hd : (k + 1) * half * hd, :],
+
+    early = jnp.dot(gathered(0), w_out[0:hw, :], preferred_element_type=jnp.float32)
+    relay(att_all.at[1], a_send.at[1], a_recv.at[1], gathers[1])
+    late = gathered(1)
+    pieces = out_rows.shape[0]
+    span = wide // pieces
+    rounds = []
+    for c in range(pieces):
+        piece = early[:, c * span : (c + 1) * span] + jnp.dot(
+            late,
+            w_out[hw : 2 * hw, c * span : (c + 1) * span],
             preferred_element_type=jnp.float32,
         )
-
-    early = project(0)
-    relay(att_all.at[1], a_send.at[1], a_recv.at[1], gathers[1])
-    out_sum = (early + project(1)).reshape(out_part.shape)
-    out_part[...] = out_sum.astype(jnp.bfloat16)
-    own_part[...] = out_sum
-    sends = []
-    for d in range(1, kvn):
-        t = lax.rem(kv + d, kvn)
-        sends.append(
-            remote(out_part.at[t], kv_part.at[d], kv_send.at[d], kv_recv.at[d], "kv", t)
-        )
-        sends[-1].start()
-    total = own_part[kv]
-    for send in sends:
+        own_part[c] = piece.reshape(kvn, quarter, span)
+        out_part[c] = own_part[c].astype(jnp.bfloat16)
+        sends = []
+        for d in range(1, kvn):
+            t = lax.rem(kv + d, kvn)
+            sends.append(
+                remote(
+                    out_part.at[c, t],
+                    kv_part.at[c, d],
+                    kv_send.at[c, d],
+                    kv_recv.at[c, d],
+                    "kv",
+                    t,
+                )
+            )
+            sends[-1].start()
+        rounds.append(sends)
+    start = pl.multiple_of(kv * quarter, 16)
+    finals = []
+    for c in range(pieces):
+        for send in rounds[c]:
+            send.wait()
+        total = own_part[c, kv]
+        for d in range(1, kvn):
+            total = total + kv_part[c, d].astype(jnp.float32)
+        residual = stream[pl.ds(start, quarter), c * span : (c + 1) * span]
+        out_rows[c, kv] = (residual + total).astype(jnp.bfloat16)
+        for d in range(1, kvn):
+            t = lax.rem(kv + d, kvn)
+            finals.append(
+                remote(
+                    out_rows.at[c, kv],
+                    out_rows.at[c, kv],
+                    o_send.at[c, d],
+                    o_recv.at[c, d],
+                    "kv",
+                    t,
+                )
+            )
+            finals[-1].start()
+    for send in finals:
         send.wait()
-    for d in range(1, kvn):
-        total = total + kv_part[d].astype(jnp.float32)
-    start = pl.multiple_of(kv * quarter, 16)
-    out_rows[kv] = (stream[pl.ds(start, quarter)] + total).astype(jnp.bfloat16)
-    sends = []
-    for d in range(1, kvn):
-        t = lax.rem(kv + d, kvn)
-        sends.append(
-            remote(out_rows.at[kv], out_rows.at[kv], o_send.at[d], o_recv.at[d], "kv", t)
-        )
-        sends[-1].start()
-    for send in sends:
-        send.wait()
-    result = out_rows[...].astype(jnp.float32).reshape(n, steps, here, wide)
-    out_ref[...] = result.transpose(1, 0, 2, 3).reshape(steps, beams, wide).astype(jnp.bfloat16)
+    for c in range(pieces):
+        result = out_rows[c].astype(jnp.float32).reshape(n, steps, here, span)
+        out_ref[:, :, c * span : (c + 1) * span] = (
+            result.transpose(1, 0, 2, 3).reshape(steps, beams, span).astype(jnp.bfloat16)
+        )
 
 
 def pick(table, index):
@@ -571,6 +600,7 @@
     total_rows = n * rows
     columns = (heads + 2) * hd
     quarter = total_rows // kvn
+    pieces = 2 if wide % 256 == 0 else 1
     sizes = (n, kvn, steps, here, heads, hd, slots, wide * n)
     bf16, f32 = jnp.bfloat16, jnp.float32
     dma = pltpu.SemaphoreType.DMA
@@ -615,10 +645,10 @@
             pltpu.VMEM((2, chips, lanes, hd), bf16),
             pltpu.VMEM((2, chips, 1, lanes), f32),
             pltpu.VMEM((2, n, lanes, hd), bf16),
-            pltpu.VMEM((kvn, quarter, wide), bf16),
-            pltpu.VMEM((kvn, quarter, wide), f32),
-            pltpu.VMEM((kvn, quarter, wide), bf16),
-            pltpu.VMEM((kvn, quarter, wide), bf16),
+            pltpu.VMEM((pieces, kvn, quarter, wide // pieces), bf16),
+            pltpu.VMEM((pieces, kvn, quarter, wide // pieces), f32),
+            pltpu.VMEM((pieces, kvn, quarter, wide // pieces), bf16),
+            pltpu.VMEM((pieces, kvn, quarter, wide // pieces), bf16),
             dma((6,)),
             dma((n,)),
             dma((n,)),
@@ -636,10 +666,10 @@
             dma((2, 2, chips)),
             dma((2, n)),
             dma((2, n)),
-            dma((kvn,)),
-            dma((kvn,)),
-            dma((kvn,)),
-            dma((kvn,)),
+            dma((pieces, kvn)),
+            dma((pieces, kvn)),
+            dma((pieces, kvn)),
+            dma((pieces, kvn)),
         ],
         compiler_params=pltpu.CompilerParams(
             collective_id=0, has_side_effects=True, vmem_limit_bytes=60 * 1024 * 1024

time: 74.3 us -> 75.3 us (1.013)
  Pallas kernels: 62 us -> 62.9 us
    pallas_call x1, Pallas kernels: 62 us -> 62.9 us  [body(): pl.pallas_call(functools.partial(kernel, sizes), out_shape=(jax.ShapeDtyp...]
where the time goes in v5:
time: 75.3 us; the launch traced here: 74.9 us
  Pallas kernels  62.9 us (84%)
  other arithmetic  5.76 us (8%)
  local copies, waits for them, and re-layouts  5.47 us (7%)
  between operations  0.77 us (1%)
    pallas_call x1, Pallas kernels, body(): pl.pallas_call(functools.partial(kernel, sizes), out_shape=(jax.ShapeDtyp...  62.9 us
    unnamed x2, local copies, waits for them, and re-layouts  2.93 us
    reduce_sum x5, other arithmetic, pick(): return jnp.sum(jnp.where(hit, table[None, :], 0), axis=1)  2.25 us
    reduce_sum x1, other arithmetic, body(): code = jnp.sum(jnp.where(named, code[None], 0), axis=(1, 2)) - 1  1.51 us

profile of v5, /device:TPU:0, one launch (start us, length us, event | category | flops | bytes accessed | tf_op | source)
XLA Modules:
  0.0 74.9 jit_solution(13260045309229514874)
XLA Ops:
  0.7 0.8 %slice_bitcast_fusion = (s32[64]{0:T(128)S(1)}, s32[64]{0:T(128)S(1)}, s32[64]{0:T(128)S(1)}) fusion(s32[3,64]{1,0:T(4,128)} %param.19), kind=kLoop, calls=%fused_computation.78 | loop fusion | bytes 1536 | tf_op jit(solution)/shard_map/eq | solution.py:533
  1.5 0.2 select_reduce_fusion.7
  1.7 0.2 select_reduce_fusion.6
  1.9 0.2 select_reduce_fusion.5
  2.1 0.1 constant_dynamic-slice_fusion
  2.2 0.1 eq.175
  2.3 0.8 %select_reduce_fusion.9 = s32[24]{0:T(128)S(1)} fusion(s32[64]{0:T(128)} %param.17, s32[24]{0:T(128)S(1)} %eq.175), kind=kLoop, calls=%fused_computation.23 | loop fusion | flops 4584 | bytes 448 | tf_op jit(solution)/shard_map/reduce_sum | solution.py:534
  3.1 0.1 add.190
  3.2 0.1 reduce_sum.150
  3.3 0.1 reduce_sum.146
  3.3 0.1 reduce_sum.148
  3.5 0.1 stack.64
  3.5 0.1 stack.63
  3.6 0.1 stack.62
  3.7 0.1 stack.69
  3.8 0.1 reshape.431
  3.9 0.7 fusion.1
  4.7 1.5 %select_reduce_fusion = s32[32]{0:T(128)S(1)} fusion(s32[64,64]{1,0:T(8,128)S(1)} %add_add_fusion, s32[64,64]{1,0:T(8,128)} %param.18, s32[32]{0:T(128)S(1)} %iota_add_fusion), kind=kLoop, calls=%fused_computation | loop fusion | flops 393184 | bytes 33024 | tf_op jit(solution)/shard_map/reduce_sum | solution.py:561
  6.2 0.8 %select_reduce_fusion.8 = s32[32]{0:T(128)S(1)} fusion(s32[64]{0:T(128)} %param.17, s32[32]{0:T(128)S(1)} %get-tuple-element.21), kind=kLoop, calls=%fused_computation.16 | loop fusion | flops 6112 | bytes 512 | tf_op jit(solution)/shard_map/reduce_sum | solution.py:534
  7.1 0.1 convert_reduce_fusion.3
  7.2 0.2 convert_reduce_fusion.1
  7.5 0.1 iota_compare_fusion.4
  7.5 0.1 select_reduce_fusion.1
  7.6 0.1 reshape.427
  7.7 0.6 pad_add_fusion.1.slot_ref
  8.3 0.7 reshape.428.info_ref
  9.1 62.9 %shard_map.113 = (bf16[3,64,512]{2,1,0:T(8,128)(2,1)}, bf16[24,256]{1,0:T(8,128)(2,1)}) custom-call(s32[176]{0:T(256)} %pad_add_fusion.1.slot_ref, bf16[3,64,512]{2,1,0:T(8,128)(2,1)} %embeds_ref.1, f32[1,512]{1,0:T(1,128)} %bitcast.48, s32[8,4,96]{2,1,0:T(4,128)} %reshape.428.info_ref, f32[24,128]{1,0:T(8,128)} %get-tuple-element.27.cos_ref, ...), custom_call_target="tpu_custom_call" | custom-call | tf_op jit(solution)/shard_map/pallas_call | solution.py:611
  72.0 1.3 %copy.18 = bf16[3,8,1,2,128]{4,3,2,1,0:T(2,128)(2,1)} copy(bf16[3,8,1,2,128]{4,1,3,0,2:T(8,128)(2,1)} %bitcast.44) | data formatting | bytes 24576
  73.3 1.6 %copy.22 = bf16[3,64,512]{2,1,0:T(8,128)(2,1)} copy(bf16[3,64,512]{2,1,0:T(8,128)(2,1)} %get-tuple-element.39) | data formatting | bytes 393216
  (20 shorter events, 0.2 us)

commit v6 on v4

--- a/solution.py
+++ b/solution.py
@@ -333,7 +333,7 @@
             seg_top[i] = top
             return top
 
-        lax.fori_loop(0, slots, look, jnp.full((1, lanes), NEGATIVE, jnp.float32), unroll=16)
+        lax.fori_loop(0, slots, look, jnp.full((1, lanes), NEGATIVE, jnp.float32), unroll=4)
         for g in range(n):
             top = jnp.where(slot_ref[5 * slots + n + g] > 0, seg_top[slot_ref[5 * slots + g]], NEGATIVE)
             tops[k, 0, g : g + 1, :] = jnp.where(me == g, jnp.maximum(top, own_top), top)
@@ -383,7 +383,7 @@
             slots,
             add,
             (jnp.zeros((hd, lanes), jnp.float32), jnp.zeros((1, lanes), jnp.float32)),
-            unroll=8,
+            unroll=4,
         )
         own_probs = jnp.exp(own_scores[k] - ceilings[me])
         own_nums.append(

time: 74.3 us -> 75.5 us (1.016)
  Pallas kernels: 62 us -> 63.2 us
    pallas_call x1, Pallas kernels: 62 us -> 63.2 us  [body(): pl.pallas_call(functools.partial(kernel, sizes), out_shape=(jax.ShapeDtyp...]
where the time goes in v6:
time: 75.5 us; the launch traced here: 75.2 us
  Pallas kernels  63.2 us (84%)
  other arithmetic  5.76 us (8%)
  local copies, waits for them, and re-layouts  5.47 us (7%)
  between operations  0.77 us (1%)
    pallas_call x1, Pallas kernels, body(): pl.pallas_call(functools.partial(kernel, sizes), out_shape=(jax.ShapeDtyp...  63.2 us
    unnamed x2, local copies, waits for them, and re-layouts  2.93 us
    reduce_sum x5, other arithmetic, pick(): return jnp.sum(jnp.where(hit, table[None, :], 0), axis=1)  2.25 us
    reduce_sum x1, other arithmetic, body(): code = jnp.sum(jnp.where(named, code[None], 0), axis=(1, 2)) - 1  1.51 us

profile of v6, /device:TPU:0, one launch (start us, length us, event | category | flops | bytes accessed | tf_op | source)
XLA Modules:
  0.0 75.2 jit_solution(8773449751200083433)
XLA Ops:
  0.7 0.8 %slice_bitcast_fusion = (s32[64]{0:T(128)S(1)}, s32[64]{0:T(128)S(1)}, s32[64]{0:T(128)S(1)}) fusion(s32[3,64]{1,0:T(4,128)} %param.19), kind=kLoop, calls=%fused_computation.78 | loop fusion | bytes 1536 | tf_op jit(solution)/shard_map/eq | solution.py:504
  1.5 0.2 select_reduce_fusion.7
  1.7 0.2 select_reduce_fusion.6
  1.9 0.2 select_reduce_fusion.5
  2.1 0.1 constant_dynamic-slice_fusion
  2.2 0.1 eq.175
  2.3 0.8 %select_reduce_fusion.9 = s32[24]{0:T(128)S(1)} fusion(s32[64]{0:T(128)} %param.17, s32[24]{0:T(128)S(1)} %eq.175), kind=kLoop, calls=%fused_computation.23 | loop fusion | flops 4584 | bytes 448 | tf_op jit(solution)/shard_map/reduce_sum | solution.py:505
  3.1 0.1 add.190
  3.2 0.1 reduce_sum.150
  3.3 0.1 reduce_sum.146
  3.3 0.1 reduce_sum.148
  3.5 0.1 stack.64
  3.5 0.1 stack.63
  3.6 0.1 stack.62
  3.7 0.1 stack.69
  3.8 0.1 reshape.431
  3.9 0.7 fusion.1
  4.7 1.5 %select_reduce_fusion = s32[32]{0:T(128)S(1)} fusion(s32[64,64]{1,0:T(8,128)S(1)} %add_add_fusion, s32[64,64]{1,0:T(8,128)} %param.18, s32[32]{0:T(128)S(1)} %iota_add_fusion), kind=kLoop, calls=%fused_computation | loop fusion | flops 393184 | bytes 33024 | tf_op jit(solution)/shard_map/reduce_sum | solution.py:532
  6.2 0.8 %select_reduce_fusion.8 = s32[32]{0:T(128)S(1)} fusion(s32[64]{0:T(128)} %param.17, s32[32]{0:T(128)S(1)} %get-tuple-element.21), kind=kLoop, calls=%fused_computation.16 | loop fusion | flops 6112 | bytes 512 | tf_op jit(solution)/shard_map/reduce_sum | solution.py:505
  7.1 0.1 convert_reduce_fusion.3
  7.2 0.2 convert_reduce_fusion.1
  7.5 0.1 iota_compare_fusion.4
  7.5 0.1 select_reduce_fusion.1
  7.6 0.1 reshape.427
  7.7 0.6 pad_add_fusion.1.slot_ref
  8.3 0.7 reshape.428.info_ref
  9.1 63.2 %shard_map.113 = (bf16[3,64,512]{2,1,0:T(8,128)(2,1)}, bf16[24,256]{1,0:T(8,128)(2,1)}) custom-call(s32[176]{0:T(256)} %pad_add_fusion.1.slot_ref, bf16[3,64,512]{2,1,0:T(8,128)(2,1)} %embeds_ref.1, f32[1,512]{1,0:T(1,128)} %bitcast.48, s32[8,4,96]{2,1,0:T(4,128)} %reshape.428.info_ref, f32[24,128]{1,0:T(8,128)} %get-tuple-element.27.cos_ref, ...), custom_call_target="tpu_custom_call" | custom-call | tf_op jit(solution)/shard_map/pallas_call | solution.py:581
  72.2 1.3 %copy.18 = bf16[3,8,1,2,128]{4,3,2,1,0:T(2,128)(2,1)} copy(bf16[3,8,1,2,128]{4,1,3,0,2:T(8,128)(2,1)} %bitcast.44) | data formatting | bytes 24576
  73.5 1.6 %copy.22 = bf16[3,64,512]{2,1,0:T(8,128)(2,1)} copy(bf16[3,64,512]{2,1,0:T(8,128)(2,1)} %get-tuple-element.39) | data formatting | bytes 393216
  (20 shorter events, 0.2 us)
